TPU v7x, 512 devices: a whole 4x4x16 slice. The times are simulated.
512 devices in a mesh: dp: 512 (over y, z, x, core).
Axes of the slice: x: 4, y: 4, z: 16, core: 2. Of those that a mesh axis runs over, the one named last changes fastest.
Arguments:
- image_embed: float32 [131072, 1152], P('dp'), may hold values from -0.1875 to 0.1875
- text_embed: float32 [131072, 1152], P('dp'), may hold values from -0.1875 to 0.1875
- logit_scale: float32 [1], replicated, may hold values from 4 to 16
- logit_bias: float32 [1], replicated, may hold values from -3 to -0.5
Outputs:
- grad_image: float32 [131072, 1152], P('dp')
- grad_text: float32 [131072, 1152], P('dp')
All inputs are finite; a program needn't handle non-finite values.
Results may differ from a plain program's by a relative error of at most 0.0001.
Values sent between devices are 32-bit elements; how exact they have to be, the bound alone decides.
No kernel may reach another device: no remote copies, remote signals or barrier semaphores. Data moves between devices by JAX's collectives and lax.ppermute only.
A program may use at most 64 MiB of HBM per device.

v0:
```python
import jax
import jax.numpy as jnp
from jax import lax
from jax.sharding import PartitionSpec as P

REACH = 2


def passed_along(shard, axis, by):
    size = lax.axis_size(axis)
    return lax.ppermute(shard, axis, [(i, (i + by) % size) for i in range(size)])


def normalize(raw):
    norm = jnp.sqrt(jnp.sum(raw * raw, axis=1, keepdims=True) + 1e-06)
    return (raw / norm, norm)


def project_back(hat, grad_hat, norm):
    inner = jnp.sum(hat * grad_hat, axis=1, keepdims=True)
    return (grad_hat - hat * inner) / norm


def fetch_band(payload):
    blocks = {0: payload}
    upper = payload
    lower = payload
    for dist in range(1, REACH + 1):
        upper = passed_along(upper, "dp", 1)
        lower = passed_along(lower, "dp", -1)
        blocks[-dist] = upper
        blocks[dist] = lower
    return blocks


def tile_coeff(left, right, scale, bias, matching):
    rows = left.shape[0]
    logits = (
        scale
        * lax.dot_general(
            left,
            right,
            (((1,), (1,)), ((), ())),
            precision=lax.Precision.HIGHEST,
            preferred_element_type=jnp.float32,
        )
        + bias
    )
    if matching:
        ident = (
            lax.broadcasted_iota(jnp.int32, (rows, rows), 0)
            == lax.broadcasted_iota(jnp.int32, (rows, rows), 1)
        ).astype(jnp.float32)
        sign = 2.0 * ident - 1.0
    else:
        sign = -jnp.ones((rows, rows), jnp.float32)
    return -sign * jax.nn.sigmoid(-sign * logits)


def apply_left(coeff, right):
    return jnp.dot(
        coeff, right, precision=lax.Precision.HIGHEST, preferred_element_type=jnp.float32
    )


def apply_trans(coeff, left):
    return lax.dot_general(
        coeff,
        left,
        (((0,), (0,)), ((), ())),
        precision=lax.Precision.HIGHEST,
        preferred_element_type=jnp.float32,
    )


def body(image_embed, text_embed, logit_scale, logit_bias):
    img_hat, img_norm = normalize(image_embed)
    txt_hat, txt_norm = normalize(text_embed)
    scale = logit_scale[0]
    bias = logit_bias[0]
    img_grad = jnp.zeros(img_hat.shape, jnp.float32)
    blocks = fetch_band(txt_hat)
    partials = {}
    for offset in range(-REACH, REACH + 1):
        coeff = tile_coeff(img_hat, blocks[offset], scale, bias, offset == 0)
        img_grad = img_grad + scale * apply_left(coeff, blocks[offset])
        partials[offset] = scale * apply_trans(coeff, img_hat)
    upward = jnp.zeros(img_hat.shape, jnp.float32)
    downward = jnp.zeros(img_hat.shape, jnp.float32)
    for dist in range(REACH, 0, -1):
        upward = passed_along(upward + partials[dist], "dp", 1)
        downward = passed_along(downward + partials[-dist], "dp", -1)
    txt_grad = partials[0] + upward + downward
    grad_image = project_back(img_hat, img_grad, img_norm)
    grad_text = project_back(txt_hat, txt_grad, txt_norm)
    return (grad_image, grad_text)


def solution(mesh):
    return jax.shard_map(
        body,
        mesh=mesh,
        in_specs=(P("dp", None), P("dp", None), P(), P()),
        out_specs=(P("dp", None), P("dp", None)),
        check_vma=False,
    )
```

profile of v0, /device:TPU:0, one launch (start us, length us, event | category | flops | bytes accessed | tf_op | source)
XLA Modules:
  0.0 107.3 jit_solution(10354242525792779908)
XLA Ops:
  0.6 0.0 copy-start.1
  0.6 1.5 %multiply_reduce_fusion.2 = f32[256]{0:T(256)S(1)} fusion(f32[256,1152]{1,0:T(8,128)} %param.5), kind=kLoop, calls=%fused_computation.17 | loop fusion | flops 589568 | bytes 1180672 | tf_op jit(solution)/shard_map/reduce_sum | solution.py:15
  2.2 0.1 copy-done.1
  2.3 0.0 copy-start
  2.3 0.1 broadcast_divide_fusion
  2.4 2.1 %collective-permute-start = (f32[256,1152]{1,0:T(8,128)S(1)}, f32[256,1152]{1,0:T(8,128)S(1)}, u32[]{:S(2)}, u32[]{:S(2)}) collective-permute-start(f32[256,1152]{1,0:T(8,128)S(1)} %broadcast_divide_fusion), channel_id=1, source_target_pairs={{0,1},{1,2},{2,3},{3,4},{4,5},{5,6},{6,7},{7,8},{8,9},{9,10},{10,1... | collective-permute-start | bytes 3538952 | tf_op jit(solution)/shard_map/ppermute | solution.py:11
  4.5 10.1 %collective-permute-start.2 = (f32[256,1152]{1,0:T(8,128)S(1)}, f32[256,1152]{1,0:T(8,128)S(1)}, u32[]{:S(2)}, u32[]{:S(2)}) collective-permute-start(f32[256,1152]{1,0:T(8,128)S(1)} %broadcast_divide_fusion), channel_id=1, source_target_pairs={{0,511},{1,0},{2,1},{3,2},{4,3},{5,4},{6,5},{7,6},{8,7},{9,8},{10,... | collective-permute-start | bytes 3538952 | tf_op jit(solution)/shard_map/ppermute | solution.py:11
  14.6 11.9 %collective-permute-done = f32[256,1152]{1,0:T(8,128)S(1)} collective-permute-done((f32[256,1152]{1,0:T(8,128)S(1)}, f32[256,1152]{1,0:T(8,128)S(1)}, u32[]{:S(2)}, u32[]{:S(2)}) %collective-permute-start) | collective-permute-done | bytes 1179680 | tf_op jit(solution)/shard_map/ppermute | solution.py:11
  26.5 1.9 %collective-permute-start.1 = (f32[256,1152]{1,0:T(8,128)S(1)}, f32[256,1152]{1,0:T(8,128)S(1)}, u32[]{:S(2)}, u32[]{:S(2)}) collective-permute-start(f32[256,1152]{1,0:T(8,128)S(1)} %collective-permute-done), channel_id=1, source_target_pairs={{0,1},{1,2},{2,3},{3,4},{4,5},{5,6},{6,7},{7,8},{8,9},{9,10},{10,1... | collective-permute-start | bytes 3538952 | tf_op jit(solution)/shard_map/ppermute | solution.py:11
  28.5 0.0 copy-done
  28.5 0.2 multiply_reduce_fusion.3
  29.9 1.3 %fusion.30 = f32[256,256]{1,0:T(8,128)S(1)} fusion(f32[256,1152]{1,0:T(8,128)S(1)} %broadcast_divide_fusion, f32[]{:T(128)} %bitcast.36, f32[]{:T(128)} %bitcast.31, f32[256,1152]{1,0:T(8,128)S(1)} %copy-done, f32[256]{0:T(256)S(1)} %add_sqrt_fusion.1), kind=kOutput, calls=%fused_computation.50 | convolution fusion | flops 906985472 | bytes 2622472 | tf_op jit(solution)/shard_map/dot_general | solution.py:40
  31.3 0.0 collective-permute-done.2
  31.3 9.1 %collective-permute-start.3 = (f32[256,1152]{1,0:T(8,128)S(1)}, f32[256,1152]{1,0:T(8,128)S(1)}, u32[]{:S(2)}, u32[]{:S(2)}) collective-permute-start(f32[256,1152]{1,0:T(8,128)S(1)} %collective-permute-done.2), channel_id=1, source_target_pairs={{0,511},{1,0},{2,1},{3,2},{4,3},{5,4},{6,5},{7,6},{8,7},{9,8},{10,... | collective-permute-start | bytes 3538952 | tf_op jit(solution)/shard_map/ppermute | solution.py:11
  40.3 1.2 %fusion.32 = f32[256,1152]{1,0:T(8,128)S(1)} fusion(f32[256,256]{1,0:T(8,128)S(1)} %fusion.30, f32[256,1152]{1,0:T(8,128)S(1)} %broadcast_divide_fusion), kind=kOutput, calls=%fused_computation.57 | convolution fusion | flops 905969664 | bytes 2621440 | tf_op jit(solution)/shard_map/dot_general | solution.py:61
  41.6 1.3 %fusion.20 = f32[256,256]{1,0:T(8,128)S(1)} fusion(f32[256,1152]{1,0:T(8,128)S(1)} %collective-permute-done, f32[]{:T(128)} %bitcast.37, f32[]{:T(128)} %bitcast.32, f32[256,1152]{1,0:T(8,128)S(1)} %copy-done, f32[256]{0:T(256)S(1)} %add_sqrt_fusion.1), kind=kOutput, calls=%fused_computation.40 | convolution fusion | flops 906592256 | bytes 2622472 | tf_op jit(solution)/shard_map/dot_general | solution.py:40
  42.9 6.6 %collective-permute-done.1 = f32[256,1152]{1,0:T(8,128)S(1)} collective-permute-done((f32[256,1152]{1,0:T(8,128)S(1)}, f32[256,1152]{1,0:T(8,128)S(1)}, u32[]{:S(2)}, u32[]{:S(2)}) %collective-permute-start.1) | collective-permute-done | bytes 1179680 | tf_op jit(solution)/shard_map/ppermute | solution.py:11
  49.5 1.3 %fusion.18 = f32[256,256]{1,0:T(8,128)S(1)} fusion(f32[256,1152]{1,0:T(8,128)S(1)} %collective-permute-done.1, f32[]{:T(128)} %bitcast.33, f32[]{:T(128)} %bitcast.23, f32[256,1152]{1,0:T(8,128)S(1)} %copy-done, f32[256]{0:T(256)S(1)} %add_sqrt_fusion.1), kind=kOutput, calls=%fused_computation.38 | convolution fusion | flops 906592256 | bytes 2622472 | tf_op jit(solution)/shard_map/dot_general | solution.py:40
  50.8 1.4 %convolution_multiply_fusion.1 = f32[256,1152]{1,0:T(8,128)S(1)} fusion(f32[256,256]{1,0:T(8,128)S(1)} %fusion.18, f32[]{:T(128)} %bitcast.27, f32[256,1152]{1,0:T(8,128)S(1)} %copy-done, f32[256]{0:T(256)S(1)} %add_sqrt_fusion.1), kind=kOutput, calls=%fused_computation.2 | convolution fusion | flops 906559488 | bytes 2622468 | tf_op jit(solution)/shard_map/dot_general | solution.py:67
  52.2 1.9 %collective-permute-start.6 = (f32[256,1152]{1,0:T(8,128)S(1)}, f32[256,1152]{1,0:T(8,128)S(1)}, u32[]{:S(2)}, u32[]{:S(2)}) collective-permute-start(f32[256,1152]{1,0:T(8,128)S(1)} %convolution_multiply_fusion.1), channel_id=1, source_target_pairs={{0,511},{1,0},{2,1},{3,2},{4,3},{5,4},{6,5},{7,6},{8,7},{9,8},{10,... | collective-permute-start | bytes 3538952 | tf_op jit(solution)/shard_map/ppermute | solution.py:11
  54.1 0.0 collective-permute-done.3
  54.1 1.3 %fusion.27 = f32[256,256]{1,0:T(8,128)S(1)} fusion(f32[256,1152]{1,0:T(8,128)S(1)} %collective-permute-done.3, f32[]{:T(128)} %bitcast.34, f32[]{:T(128)} %bitcast.29, f32[256,1152]{1,0:T(8,128)S(1)} %copy-done, f32[256]{0:T(256)S(1)} %add_sqrt_fusion.1), kind=kOutput, calls=%fused_computation.47 | convolution fusion | flops 906592256 | bytes 2622472 | tf_op jit(solution)/shard_map/dot_general | solution.py:40
  55.4 1.4 %convolution_multiply_fusion.3 = f32[256,1152]{1,0:T(8,128)S(1)} fusion(f32[256,256]{1,0:T(8,128)S(1)} %fusion.27, f32[]{:T(128)} %bitcast.25, f32[256,1152]{1,0:T(8,128)S(1)} %copy-done, f32[256]{0:T(256)S(1)} %add_sqrt_fusion.1), kind=kOutput, calls=%fused_computation.5 | convolution fusion | flops 906559488 | bytes 2622468 | tf_op jit(solution)/shard_map/dot_general | solution.py:67
  56.8 2.6 %collective-permute-start.4 = (f32[256,1152]{1,0:T(8,128)S(1)}, f32[256,1152]{1,0:T(8,128)S(1)}, u32[]{:S(2)}, u32[]{:S(2)}) collective-permute-start(f32[256,1152]{1,0:T(8,128)S(1)} %convolution_multiply_fusion.3), channel_id=1, source_target_pairs={{0,1},{1,2},{2,3},{3,4},{4,5},{5,6},{6,7},{7,8},{8,9},{9,10},{10,1... | collective-permute-start | bytes 3538952 | tf_op jit(solution)/shard_map/ppermute | solution.py:11
  59.4 1.2 %fusion.31 = f32[256,1152]{1,0:T(8,128)S(1)} fusion(f32[256,256]{1,0:T(8,128)S(1)} %fusion.20, f32[256,1152]{1,0:T(8,128)S(1)} %collective-permute-done), kind=kOutput, calls=%fused_computation.56 | convolution fusion | flops 905969664 | bytes 2621440 | tf_op jit(solution)/shard_map/dot_general | solution.py:61
  60.7 1.3 %fusion.25 = f32[256,256]{1,0:T(8,128)S(1)} fusion(f32[256,1152]{1,0:T(8,128)S(1)} %collective-permute-done.2, f32[]{:T(128)} %bitcast.35, f32[]{:T(128)} %bitcast.30, f32[256,1152]{1,0:T(8,128)S(1)} %copy-done, f32[256]{0:T(256)S(1)} %add_sqrt_fusion.1), kind=kOutput, calls=%fused_computation.45 | convolution fusion | flops 906592256 | bytes 2622472 | tf_op jit(solution)/shard_map/dot_general | solution.py:40
  62.0 1.3 %fusion.3 = f32[256,1152]{1,0:T(8,128)S(1)} fusion(f32[256,1152]{1,0:T(8,128)S(1)} %fusion.32, f32[256,1152]{1,0:T(8,128)S(1)} %fusion.31, f32[256,256]{1,0:T(8,128)S(1)} %fusion.18, f32[256,1152]{1,0:T(8,128)S(1)} %collective-permute-done.1), kind=kOutput, calls=%fused_computation.11 | convolution fusion | flops 906559488 | bytes 4980736 | tf_op jit(solution)/shard_map/dot_general | solution.py:61
  63.3 4.5 %collective-permute-done.6 = f32[256,1152]{1,0:T(8,128)S(1)} collective-permute-done((f32[256,1152]{1,0:T(8,128)S(1)}, f32[256,1152]{1,0:T(8,128)S(1)}, u32[]{:S(2)}, u32[]{:S(2)}) %collective-permute-start.6) | collective-permute-done | bytes 1179680 | tf_op jit(solution)/shard_map/ppermute | solution.py:11
  67.8 1.4 %fusion = f32[256,1152]{1,0:T(8,128)S(1)} fusion(f32[256,1152]{1,0:T(8,128)S(1)} %collective-permute-done.6, f32[256,256]{1,0:T(8,128)S(1)} %fusion.20, f32[]{:T(128)} %bitcast.28, f32[256,1152]{1,0:T(8,128)S(1)} %copy-done, f32[256]{0:T(256)S(1)} %add_sqrt_fusion.1), kind=kOutput, calls=%fused_computation.1 | convolution fusion | flops 906854400 | bytes 3802116 | tf_op jit(solution)/shard_map/dot_general | solution.py:67
  69.3 9.2 %collective-permute-start.7 = (f32[256,1152]{1,0:T(8,128)S(1)}, f32[256,1152]{1,0:T(8,128)S(1)}, u32[]{:S(2)}, u32[]{:S(2)}) collective-permute-start(f32[256,1152]{1,0:T(8,128)S(1)} %fusion), channel_id=1, source_target_pairs={{0,511},{1,0},{2,1},{3,2},{4,3},{5,4},{6,5},{7,6},{8,7},{9,8},{10,... | collective-permute-start | bytes 3538952 | tf_op jit(solution)/shard_map/ppermute | solution.py:11
  78.5 1.3 %collective-permute-done.4 = f32[256,1152]{1,0:T(8,128)S(1)} collective-permute-done((f32[256,1152]{1,0:T(8,128)S(1)}, f32[256,1152]{1,0:T(8,128)S(1)}, u32[]{:S(2)}, u32[]{:S(2)}) %collective-permute-start.4) | collective-permute-done | bytes 1179680 | tf_op jit(solution)/shard_map/ppermute | solution.py:11
  79.9 1.4 %fusion.1 = f32[256,1152]{1,0:T(8,128)S(1)} fusion(f32[256,1152]{1,0:T(8,128)S(1)} %collective-permute-done.4, f32[256,256]{1,0:T(8,128)S(1)} %fusion.25, f32[]{:T(128)} %bitcast.26, f32[256,1152]{1,0:T(8,128)S(1)} %copy-done, f32[256]{0:T(256)S(1)} %add_sqrt_fusion.1), kind=kOutput, calls=%fused_computation.4 | convolution fusion | flops 906854400 | bytes 3802116 | tf_op jit(solution)/shard_map/dot_general | solution.py:67
  81.3 1.9 %collective-permute-start.5 = (f32[256,1152]{1,0:T(8,128)S(1)}, f32[256,1152]{1,0:T(8,128)S(1)}, u32[]{:S(2)}, u32[]{:S(2)}) collective-permute-start(f32[256,1152]{1,0:T(8,128)S(1)} %fusion.1), channel_id=1, source_target_pairs={{0,1},{1,2},{2,3},{3,4},{4,5},{5,6},{6,7},{7,8},{8,9},{9,10},{10,1... | collective-permute-start | bytes 3538952 | tf_op jit(solution)/shard_map/ppermute | solution.py:11
  83.2 1.3 %convolution_add_fusion.1 = f32[256,1152]{1,0:T(8,128)S(1)} fusion(f32[256,1152]{1,0:T(8,128)S(1)} %fusion.3, f32[256,256]{1,0:T(8,128)S(1)} %fusion.25, f32[256,1152]{1,0:T(8,128)S(1)} %collective-permute-done.2), kind=kOutput, calls=%fused_computation.9 | convolution fusion | flops 906264576 | bytes 3801088 | tf_op jit(solution)/shard_map/dot_general | solution.py:61
  84.5 1.5 %multiply_reduce_fusion.1 = (f32[256]{0:T(256)S(1)}, f32[256,1152]{1,0:T(8,128)S(1)}) fusion(f32[256,1152]{1,0:T(8,128)S(1)} %copy-done, f32[256]{0:T(256)S(1)} %add_sqrt_fusion.1, f32[]{:T(128)} %bitcast.22, f32[256,1152]{1,0:T(8,128)S(1)} %convolution_add_fusion.1, f32[256,256]{1,0:T(8,128)S(1)} %fusion.27, f32[256,1152]{1,0:T(8,128)S(1)} %collective-permute-done.3), kind=kOutput, calls=%fused_computation.16 | convolution fusion | flops 907443968 | bytes 4982788 | tf_op jit(solution)/shard_map/dot_general | solution.py:61
  86.0 1.3 %subtract_divide_fusion.1 = f32[256,1152]{1,0:T(8,128)} fusion(f32[256,1152]{1,0:T(8,128)S(1)} %get-tuple-element.3, f32[256]{0:T(256)S(1)} %get-tuple-element.2, f32[256]{0:T(256)S(1)} %add_sqrt_fusion.1, f32[256,1152]{1,0:T(8,128)S(1)} %copy-done), kind=kLoop, calls=%fused_computation.15 | loop fusion | flops 1179648 | bytes 3540992 | tf_op jit(solution)/shard_map/div | solution.py:21
  87.3 4.9 %collective-permute-done.7 = f32[256,1152]{1,0:T(8,128)S(1)} collective-permute-done((f32[256,1152]{1,0:T(8,128)S(1)}, f32[256,1152]{1,0:T(8,128)S(1)}, u32[]{:S(2)}, u32[]{:S(2)}) %collective-permute-start.7) | collective-permute-done | bytes 1179680 | tf_op jit(solution)/shard_map/ppermute | solution.py:11
  92.2 12.0 %collective-permute-done.5 = f32[256,1152]{1,0:T(8,128)S(1)} collective-permute-done((f32[256,1152]{1,0:T(8,128)S(1)}, f32[256,1152]{1,0:T(8,128)S(1)}, u32[]{:S(2)}, u32[]{:S(2)}) %collective-permute-start.5) | collective-permute-done | bytes 1179680 | tf_op jit(solution)/shard_map/ppermute | solution.py:11
  104.3 1.7 %multiply_reduce_fusion = (f32[256]{0:T(256)S(1)}, f32[256,1152]{1,0:T(8,128)S(1)}) fusion(f32[256,1152]{1,0:T(8,128)S(1)} %broadcast_divide_fusion, f32[256,1152]{1,0:T(8,128)S(1)} %collective-permute-done.7, f32[256,1152]{1,0:T(8,128)S(1)} %collective-permute-done.5, f32[256,256]{1,0:T(8,128)S(1)} %fusion.30, f32[256,1152]{1,0:T(8,128)S(1)} %copy-done, ...), kind=kOutput, calls=%fused_computation.13 | convolution fusion | flops 907738880 | bytes 6162436 | tf_op jit(solution)/shard_map/dot_general | solution.py:67
  106.0 1.3 %subtract_divide_fusion = f32[256,1152]{1,0:T(8,128)} fusion(f32[256]{0:T(256)S(1)} %get-tuple-element.4, f32[256]{0:T(256)S(1)} %add_sqrt_fusion, f32[256,1152]{1,0:T(8,128)S(1)} %collective-permute-done.7, f32[256,1152]{1,0:T(8,128)S(1)} %get-tuple-element.5, f32[256,1152]{1,0:T(8,128)S(1)} %collective-permute-done.5, f32[256,1152]{1,0:T(8,128)S(1)} %copy-done.1), kind=kLoop, calls=%fused_computation.12 | loop fusion | flops 1769472 | bytes 5900288 | tf_op jit(solution)/shard_map/div | solution.py:21
  (2 shorter events, 0.0 us)
Async XLA Ops:
  0.6 1.6 %copy-start.1 = (f32[256,1152]{1,0:T(8,128)S(1)}, f32[256,1152]{1,0:T(8,128)}, u32[]{:S(2)}) copy-start(f32[256,1152]{1,0:T(8,128)} %param.5) | copy-start | bytes 3538948
  2.3 26.2 %copy-start = (f32[256,1152]{1,0:T(8,128)S(1)}, f32[256,1152]{1,0:T(8,128)}, u32[]{:S(2)}) copy-start(f32[256,1152]{1,0:T(8,128)} %param.4) | copy-start | bytes 3538948
  2.4 24.1 %collective-permute-start = (f32[256,1152]{1,0:T(8,128)S(1)}, f32[256,1152]{1,0:T(8,128)S(1)}, u32[]{:S(2)}, u32[]{:S(2)}) collective-permute-start(f32[256,1152]{1,0:T(8,128)S(1)} %broadcast_divide_fusion), channel_id=1, source_target_pairs={{0,1},{1,2},{2,3},{3,4},{4,5},{5,6},{6,7},{7,8},{8,9},{9,10},{10,1... | collective-permute-start | bytes 3538952 | tf_op jit(solution)/shard_map/ppermute | solution.py:11
  4.5 26.8 %collective-permute-start.2 = (f32[256,1152]{1,0:T(8,128)S(1)}, f32[256,1152]{1,0:T(8,128)S(1)}, u32[]{:S(2)}, u32[]{:S(2)}) collective-permute-start(f32[256,1152]{1,0:T(8,128)S(1)} %broadcast_divide_fusion), channel_id=1, source_target_pairs={{0,511},{1,0},{2,1},{3,2},{4,3},{5,4},{6,5},{7,6},{8,7},{9,8},{10,... | collective-permute-start | bytes 3538952 | tf_op jit(solution)/shard_map/ppermute | solution.py:11
  26.5 22.9 %collective-permute-start.1 = (f32[256,1152]{1,0:T(8,128)S(1)}, f32[256,1152]{1,0:T(8,128)S(1)}, u32[]{:S(2)}, u32[]{:S(2)}) collective-permute-start(f32[256,1152]{1,0:T(8,128)S(1)} %collective-permute-done), channel_id=1, source_target_pairs={{0,1},{1,2},{2,3},{3,4},{4,5},{5,6},{6,7},{7,8},{8,9},{9,10},{10,1... | collective-permute-start | bytes 3538952 | tf_op jit(solution)/shard_map/ppermute | solution.py:11
  31.3 22.9 %collective-permute-start.3 = (f32[256,1152]{1,0:T(8,128)S(1)}, f32[256,1152]{1,0:T(8,128)S(1)}, u32[]{:S(2)}, u32[]{:S(2)}) collective-permute-start(f32[256,1152]{1,0:T(8,128)S(1)} %collective-permute-done.2), channel_id=1, source_target_pairs={{0,511},{1,0},{2,1},{3,2},{4,3},{5,4},{6,5},{7,6},{8,7},{9,8},{10,... | collective-permute-start | bytes 3538952 | tf_op jit(solution)/shard_map/ppermute | solution.py:11
  52.2 15.6 %collective-permute-start.6 = (f32[256,1152]{1,0:T(8,128)S(1)}, f32[256,1152]{1,0:T(8,128)S(1)}, u32[]{:S(2)}, u32[]{:S(2)}) collective-permute-start(f32[256,1152]{1,0:T(8,128)S(1)} %convolution_multiply_fusion.1), channel_id=1, source_target_pairs={{0,511},{1,0},{2,1},{3,2},{4,3},{5,4},{6,5},{7,6},{8,7},{9,8},{10,... | collective-permute-start | bytes 3538952 | tf_op jit(solution)/shard_map/ppermute | solution.py:11
  56.8 23.0 %collective-permute-start.4 = (f32[256,1152]{1,0:T(8,128)S(1)}, f32[256,1152]{1,0:T(8,128)S(1)}, u32[]{:S(2)}, u32[]{:S(2)}) collective-permute-start(f32[256,1152]{1,0:T(8,128)S(1)} %convolution_multiply_fusion.3), channel_id=1, source_target_pairs={{0,1},{1,2},{2,3},{3,4},{4,5},{5,6},{6,7},{7,8},{8,9},{9,10},{10,1... | collective-permute-start | bytes 3538952 | tf_op jit(solution)/shard_map/ppermute | solution.py:11
  69.3 23.0 %collective-permute-start.7 = (f32[256,1152]{1,0:T(8,128)S(1)}, f32[256,1152]{1,0:T(8,128)S(1)}, u32[]{:S(2)}, u32[]{:S(2)}) collective-permute-start(f32[256,1152]{1,0:T(8,128)S(1)} %fusion), channel_id=1, source_target_pairs={{0,511},{1,0},{2,1},{3,2},{4,3},{5,4},{6,5},{7,6},{8,7},{9,8},{10,... | collective-permute-start | bytes 3538952 | tf_op jit(solution)/shard_map/ppermute | solution.py:11
  81.3 23.0 %collective-permute-start.5 = (f32[256,1152]{1,0:T(8,128)S(1)}, f32[256,1152]{1,0:T(8,128)S(1)}, u32[]{:S(2)}, u32[]{:S(2)}) collective-permute-start(f32[256,1152]{1,0:T(8,128)S(1)} %fusion.1), channel_id=1, source_target_pairs={{0,1},{1,2},{2,3},{3,4},{4,5},{5,6},{6,7},{7,8},{8,9},{9,10},{10,1... | collective-permute-start | bytes 3538952 | tf_op jit(solution)/shard_map/ppermute | solution.py:11
where the time goes:
time: 108 us; the launch traced here: 107 us
  waiting for transfers between devices  41.3 us (38%)
  starting transfers between devices  38.8 us (36%)
  matrix products  20.5 us (19%)
  other arithmetic  4.45 us (4%)
  between operations  2.14 us (2%)
    ppermute x8, waiting for transfers between devices, passed_along(): lax.ppermute(shard, axis, [(i, (i + by) % size) for i in range(size)])  41.3 us
    ppermute x8, starting transfers between devices, passed_along(): lax.ppermute(shard, axis, [(i, (i + by) % size) for i in range(size)])  38.8 us
    dot_general x5, matrix products, apply_trans(): lax.dot_general(coeff, left, (((0,), (0,)), ((), ())), precision=lax.Prec...  7.38 us
    dot_general x5, matrix products, apply_left(): jnp.dot(coeff, right, precision=lax.Precision.HIGHEST, preferred_element_...  6.59 us
    dot_general x5, matrix products, tile_coeff(): lax.dot_general(left, right, (((1,), (1,)), ((), ())), precision=lax.Prec...  6.5 us
    div x2, other arithmetic, project_back(): return (grad_hat - hat * inner) / norm  2.61 us
  transfers between devices with their start and end apart: 8, of which 6 were waited for; matrix products, arithmetic and copies ran while one was open for 19% of the time, Pallas kernels for 0%

commit v1 on v0

v1 whole, which is shorter than its diff:
```python
import functools

import jax
import jax.numpy as jnp
from jax import lax
from jax.experimental import pallas as pl
from jax.experimental.pallas import tpu as pltpu
from jax.sharding import PartitionSpec as P

F32 = jnp.float32
BF16 = jnp.bfloat16
VMEM = pl.BlockSpec(memory_space=pltpu.VMEM)
SMEM = pl.BlockSpec(memory_space=pltpu.SMEM)
NT = (((1,), (1,)), ((), ()))
NN = (((1,), (0,)), ((), ()))


def split(value):
    hi = value.astype(BF16)
    return hi, (value - hi.astype(F32)).astype(BF16)


def product(left, right, dims):
    mul = functools.partial(
        lax.dot_general, dimension_numbers=dims, preferred_element_type=F32
    )
    (lh, ll), (rh, rl) = left, right
    return mul(lh, rh) + (mul(lh, rl) + mul(ll, rh))


def unit(raw):
    inv = 1.0 / jnp.sqrt(jnp.sum(raw * raw, axis=1, keepdims=True) + 1e-06)
    return raw * inv, inv


def tile_grad(x, y, scale, bias, matching=False):
    logits = scale * product(x, y, NT) + bias
    if matching:
        diag = lax.broadcasted_iota(jnp.int32, logits.shape, 0) == (
            lax.broadcasted_iota(jnp.int32, logits.shape, 1)
        )
        sign = jnp.where(diag, -1.0, 1.0)
        coeff = sign * jax.nn.sigmoid(sign * logits)
    else:
        coeff = jax.nn.sigmoid(logits)
    return product(split(coeff), y, NN)


def own_kernel(scale, bias, img, txt, ihat, that, ihat_a, ihat_b, stack, *outs):
    (iinv, ihi, ilo, igrad, tinv, thi, tlo, tgrad) = outs
    rows, first = img.shape[0], ihat_a.shape[0]
    stack[:rows], iinv[...] = unit(img[...])
    stack[rows:], tinv[...] = unit(txt[...])
    ihat_a[...] = stack[:first]
    ihat_b[...] = stack[first:rows]
    ihat[...] = stack[:rows]
    that[...] = stack[rows:]
    ihi[...], ilo[...] = split(stack[:rows])
    thi[...], tlo[...] = split(stack[rows:])
    x, y = (ihi[...], ilo[...]), (thi[...], tlo[...])
    igrad[...] = tile_grad(x, y, scale[0], bias[0], True)
    tgrad[...] = tile_grad(y, x, scale[0], bias[0], True)


def raw_kernel(scale, bias, hi, lo, raw, grad, hat, total):
    hat[...] = unit(raw[...])[0]
    total[...] = grad[...] + tile_grad(
        (hi[...], lo[...]), split(hat[...]), scale[0], bias[0]
    )


def tile_kernel(scale, bias, hi, lo, hat, grad, total):
    total[...] = grad[...] + tile_grad(
        (hi[...], lo[...]), split(hat[...]), scale[0], bias[0]
    )


def stack_kernel(scale, bias, hi, lo, img, txt, grad, stack, total):
    stack[: img.shape[0]] = img[...]
    stack[img.shape[0] :] = txt[...]
    tile_kernel(scale, bias, hi, lo, img, grad, total)


def pair_kernel(scale, bias, ihi, ilo, thi, tlo, stack, igrad, tgrad, itotal, ttotal):
    rows = igrad.shape[0]
    tile_kernel(scale, bias, ihi, ilo, stack.at[rows:], igrad, itotal)
    tile_kernel(scale, bias, thi, tlo, stack.at[:rows], tgrad, ttotal)


def project(out, total, hat, inv):
    inner = jnp.sum(hat * total, axis=1, keepdims=True)
    out[...] = (total - hat * inner) * inv


def cross_kernel(
    scale, bias, ihi, ilo, thi, tlo, stack, igrad, tgrad, own, iinv, out, ttotal
):
    rows = igrad.shape[0]
    y = split(stack[rows:])
    total = igrad[...] + tile_grad((ihi[...], ilo[...]), y, scale[0], bias[0])
    project(out, scale[0] * total, own[:rows], iinv[...])
    tile_kernel(scale, bias, thi, tlo, stack.at[:rows], tgrad, ttotal)


def last_kernel(scale, bias, hi, lo, hat, grad, own, inv, out):
    y = split(hat[...])
    total = grad[...] + tile_grad((hi[...], lo[...]), y, scale[0], bias[0])
    project(out, scale[0] * total, own[...], inv[...])


def call(kernel, name, operands, outs, flops=1):
    return pl.pallas_call(
        kernel,
        name=name,
        out_shape=outs,
        in_specs=[SMEM, SMEM] + [VMEM] * (len(operands) - 2),
        out_specs=jax.tree.map(lambda _: VMEM, outs),
        compiler_params=pltpu.CompilerParams(vmem_limit_bytes=24 * 2**20),
        cost_estimate=pl.CostEstimate(flops=flops, bytes_accessed=0, transcendentals=0),
    )(*operands)


def body(image_embed, text_embed, logit_scale, logit_bias):
    rows, width = image_embed.shape
    first = rows // 2
    size = lax.axis_size("dp")

    def shape(height, wide=width, kind=F32):
        return jax.ShapeDtypeStruct((height, wide), kind)

    one, both = shape(rows), shape(2 * rows)
    state = (shape(rows, 1), shape(rows, kind=BF16), shape(rows, kind=BF16), one)
    tb = (logit_scale, logit_bias)

    def outward(block):
        return lax.ppermute(
            block, "dp", [(d, (d + (2 if d % 2 else -2)) % size) for d in range(size)]
        )

    def inward(block):
        return lax.ppermute(
            block, "dp", [(d, (d + (-2 if d % 2 else 2)) % size) for d in range(size)]
        )

    def swap(block):
        return lax.ppermute(block, "dp", [(d, d ^ 1) for d in range(size)])

    def after(*values):
        return lax.optimization_barrier(values)

    near_txt = outward(text_embed)
    ihat, that, ihat_a, ihat_b, own, *rest = call(
        own_kernel,
        "own_tiles",
        (*tb, image_embed, text_embed),
        (one, one, shape(first), shape(rows - first), both, *state, *state),
    )
    iinv, ihi, ilo, igrad, tinv, thi, tlo, tgrad = rest
    img, txt = (ihi, ilo), (thi, tlo)
    pair = swap(own)
    near_img = outward(ihat)
    far_txt = inward(that)

    near_txt, igrad = call(
        raw_kernel, "near_text", (*tb, *img, near_txt, igrad), (one, one), 10**11
    )
    ihat_a, igrad = after(ihat_a, igrad)
    far_img_a = inward(ihat_a)
    igrad, tgrad = call(
        pair_kernel, "pair_tiles", (*tb, *img, *txt, pair, igrad, tgrad), (one, one)
    )
    cross, tgrad = call(
        stack_kernel, "near_image", (*tb, *txt, near_img, near_txt, tgrad), (both, one)
    )
    ihat_b, tgrad = after(ihat_b, tgrad)
    cross = swap(cross)
    far_img_b = inward(ihat_b)
    igrad, tgrad = after(igrad, tgrad)
    igrad = call(tile_kernel, "far_text", (*tb, *img, far_txt, igrad), one)
    igrad, tgrad = after(igrad, tgrad)
    tgrad = call(tile_kernel, "far_image", (*tb, *txt, far_img_a, tgrad), one, 10**11)
    grad_image, tgrad = call(
        cross_kernel,
        "cross_tiles",
        (*tb, *img, *txt, cross, igrad, tgrad, own, iinv),
        (one, one),
    )
    grad_text = call(
        last_kernel, "last_image", (*tb, *txt, far_img_b, tgrad, that, tinv), one
    )
    return grad_image, grad_text


def solution(mesh):
    return jax.shard_map(
        body,
        mesh=mesh,
        in_specs=(P("dp", None), P("dp", None), P(), P()),
        out_specs=(P("dp", None), P("dp", None)),
        check_vma=False,
    )
```

time: 108 us -> 81.4 us (0.75)
  the two profiles are of different devices: /device:TPU:0 before, /device:TPU:1 now
where the time goes in v1:
time: 81.4 us; the launch traced here: 81 us
  starting transfers between devices  47.2 us (58%)
  Pallas kernels  25.7 us (32%)
  waiting for transfers between devices  3.54 us (4%)
  local copies, waits for them, and re-layouts  2.53 us (3%)
  between operations  2.06 us (3%)
    ppermute x2, starting transfers between devices, swap(): return lax.ppermute(block, 'dp', [(d, d ^ 1) for d in range(size)])  26.2 us
    pallas_call x8, Pallas kernels, call(): pl.pallas_call(kernel, name=name, out_shape=outs, in_specs=[SMEM, SMEM] +...  25.7 us
    ppermute x3, starting transfers between devices, inward(): lax.ppermute(block, 'dp', [(d, (d + (-2 if d % 2 else 2)) % size) for d i...  13.9 us
    ppermute x2, starting transfers between devices, outward(): lax.ppermute(block, 'dp', [(d, (d + (2 if d % 2 else -2)) % size) for d i...  7.07 us
    ppermute x2, waiting for transfers between devices, outward(): lax.ppermute(block, 'dp', [(d, (d + (2 if d % 2 else -2)) % size) for d i...  3.1 us
    unnamed x4, local copies, waits for them, and re-layouts  2.53 us
  transfers between devices with their start and end apart: 7, of which 2 were waited for; matrix products, arithmetic and copies ran while one was open for 0% of the time, Pallas kernels for 28%

profile of v1, /device:TPU:1, one launch (start us, length us, event | category | flops | bytes accessed | tf_op | source)
XLA Modules:
  0.0 81.0 jit_solution(18383938398665557314)
XLA Ops:
  0.6 3.9 %collective-permute-start.1 = (f32[256,1152]{1,0:T(8,128)}, f32[256,1152]{1,0:T(8,128)S(1)}, u32[]{:S(2)}, u32[]{:S(2)}) collective-permute-start(f32[256,1152]{1,0:T(8,128)} %txt.1), channel_id=1, source_target_pairs={{0,510},{1,3},{2,0},{3,5},{4,2},{5,7},{6,4},{7,9},{8,6},{9,11},{10... | collective-permute-start | bytes 3538952 | tf_op jit(solution)/shard_map/ppermute | solution.py:136
  5.9 0.0 copy-start
  5.9 1.3 %copy-done = f32[256,1152]{1,0:T(8,128)S(1)} copy-done((f32[256,1152]{1,0:T(8,128)S(1)}, f32[256,1152]{1,0:T(8,128)}, u32[]{:S(2)}) %copy-start) | copy-done | bytes 1179672
  7.1 0.0 copy-start.1
  7.2 1.3 %copy-done.1 = f32[256,1152]{1,0:T(8,128)S(1)} copy-done((f32[256,1152]{1,0:T(8,128)S(1)}, f32[256,1152]{1,0:T(8,128)}, u32[]{:S(2)}) %copy-start.1) | copy-done | bytes 1179672
  8.4 4.9 %own_tiles.1 = (f32[256,1152]{1,0:T(8,128)S(1)}, f32[256,1152]{1,0:T(8,128)S(1)}, f32[128,1152]{1,0:T(8,128)S(1)}, f32[128,1152]{1,0:T(8,128)S(1)}, f32[512,1152...) custom-call(f32[1]{0:T(128)S(6)} %copy.6.scale, ...), custom_call_target="tpu_custom_call" | custom-call | flops 1 | tf_op jit(solution)/shard_map/own_tiles/pallas_call | solution.py:112
  13.3 3.1 %collective-permute-start = (f32[256,1152]{1,0:T(8,128)S(1)}, f32[256,1152]{1,0:T(8,128)S(1)}, u32[]{:S(2)}, u32[]{:S(2)}) collective-permute-start(f32[256,1152]{1,0:T(8,128)S(1)} %get-tuple-element.35), channel_id=1, source_target_pairs={{0,510},{1,3},{2,0},{3,5},{4,2},{5,7},{6,4},{7,9},{8,6},{9,11},{10... | collective-permute-start | bytes 3538952 | tf_op jit(solution)/shard_map/ppermute | solution.py:136
  16.4 15.1 %collective-permute-start.2 = (f32[512,1152]{1,0:T(8,128)S(1)}, f32[512,1152]{1,0:T(8,128)S(1)}, u32[]{:S(2)}, u32[]{:S(2)}) collective-permute-start(f32[512,1152]{1,0:T(8,128)S(1)} %get-tuple-element.38.own), channel_id=1, source_target_pairs={{0,1},{1,0},{2,3},{3,2},{4,5},{5,4},{6,7},{7,6},{8,9},{9,8},{10,11... | collective-permute-start | bytes 7077896 | tf_op jit(solution)/shard_map/ppermute | solution.py:146
  31.5 2.2 %collective-permute-start.4 = (f32[256,1152]{1,0:T(8,128)S(1)}, f32[256,1152]{1,0:T(8,128)S(1)}, u32[]{:S(2)}, u32[]{:S(2)}) collective-permute-start(f32[256,1152]{1,0:T(8,128)S(1)} %get-tuple-element.45.own), channel_id=1, source_target_pairs={{0,2},{1,511},{2,4},{3,1},{4,6},{5,3},{6,8},{7,5},{8,10},{9,7},{10... | collective-permute-start | bytes 3538952 | tf_op jit(solution)/shard_map/ppermute | solution.py:141
  33.7 0.0 collective-permute-done.1.raw
  33.7 2.4 %near_text.1 = (f32[256,1152]{1,0:T(8,128)S(1)}, f32[256,1152]{1,0:T(8,128)S(1)}) custom-call(f32[1]{0:T(128)S(6)} %copy.6.scale, f32[1]{0:T(128)S(6)} %copy.7.bias, bf16[256,1152]{1,0:T(8,128)(2,1)S(1)} %get-tuple-element.31.hi.ihi, bf16[256,1152]{1,0:T(8,128)(2,1)S(1)} %get-tuple-element.32.lo.ilo, f32[256,1152]{1,0:T(8,128)S(1)} %collective-permute-done.1.raw, ...), custom_call_target="tpu_custom_call" | custom-call | flops 99999997952 | tf_op jit(solution)/shard_map/near_text/pallas_call | solution.py:112
  36.2 2.2 %collective-permute-start.5 = (f32[128,1152]{1,0:T(8,128)S(1)}, f32[128,1152]{1,0:T(8,128)S(1)}, u32[]{:S(2)}, u32[]{:S(2)}) collective-permute-start(f32[128,1152]{1,0:T(8,128)S(1)} %get-tuple-element.53), channel_id=1, source_target_pairs={{0,2},{1,511},{2,4},{3,1},{4,6},{5,3},{6,8},{7,5},{8,10},{9,7},{10... | collective-permute-start | bytes 1769480 | tf_op jit(solution)/shard_map/ppermute | solution.py:141
  38.3 0.0 collective-permute-done.2.stack
  38.3 4.4 %pair_tiles.1 = (f32[256,1152]{1,0:T(8,128)S(1)}, f32[256,1152]{1,0:T(8,128)S(1)}) custom-call(f32[1]{0:T(128)S(6)} %copy.6.scale, f32[1]{0:T(128)S(6)} %copy.7.bias, bf16[256,1152]{1,0:T(8,128)(2,1)S(1)} %get-tuple-element.31.hi.ihi, bf16[256,1152]{1,0:T(8,128)(2,1)S(1)} %get-tuple-element.32.lo.ilo, bf16[256,1152]{1,0:T(8,128)(2,1)S(1)} %get-tuple-element.33.thi.hi, ...), custom_call_target="tpu_custom_call" | custom-call | flops 1 | tf_op jit(solution)/shard_map/pair_tiles/pallas_call | solution.py:112
  42.7 3.1 %collective-permute-done.img = f32[256,1152]{1,0:T(8,128)S(1)} collective-permute-done((f32[256,1152]{1,0:T(8,128)S(1)}, f32[256,1152]{1,0:T(8,128)S(1)}, u32[]{:S(2)}, u32[]{:S(2)}) %collective-permute-start) | collective-permute-done | bytes 1179680 | tf_op jit(solution)/shard_map/ppermute | solution.py:136
  45.8 2.4 %near_image.1 = (f32[512,1152]{1,0:T(8,128)S(1)}, f32[256,1152]{1,0:T(8,128)S(1)}) custom-call(f32[1]{0:T(128)S(6)} %copy.6.scale, f32[1]{0:T(128)S(6)} %copy.7.bias, bf16[256,1152]{1,0:T(8,128)(2,1)S(1)} %get-tuple-element.33.thi.hi, bf16[256,1152]{1,0:T(8,128)(2,1)S(1)} %get-tuple-element.34.tlo.lo, f32[256,1152]{1,0:T(8,128)S(1)} %collective-permute-done.img, ...), custom_call_target="tpu_custom_call" | custom-call | flops 1 | tf_op jit(solution)/shard_map/near_image/pallas_call | solution.py:112
  48.2 11.1 %collective-permute-start.3 = (f32[512,1152]{1,0:T(8,128)S(1)}, f32[512,1152]{1,0:T(8,128)S(1)}, u32[]{:S(2)}, u32[]{:S(2)}) collective-permute-start(f32[512,1152]{1,0:T(8,128)S(1)} %get-tuple-element.44), channel_id=1, source_target_pairs={{0,1},{1,0},{2,3},{3,2},{4,5},{5,4},{6,7},{7,6},{8,9},{9,8},{10,11... | collective-permute-start | bytes 7077896 | tf_op jit(solution)/shard_map/ppermute | solution.py:146
  59.3 0.0 collective-permute-done.4.hat
  59.4 2.3 %far_text.1.igrad = f32[256,1152]{1,0:T(8,128)S(1)} custom-call(f32[1]{0:T(128)S(6)} %copy.6.scale, f32[1]{0:T(128)S(6)} %copy.7.bias, bf16[256,1152]{1,0:T(8,128)(2,1)S(1)} %get-tuple-element.31.hi.ihi, bf16[256,1152]{1,0:T(8,128)(2,1)S(1)} %get-tuple-element.32.lo.ilo, f32[256,1152]{1,0:T(8,128)S(1)} %collective-permute-done.4.hat, ...), custom_call_target="tpu_custom_call" | custom-call | flops 1 | tf_op jit(solution)/shard_map/far_text/pallas_call | solution.py:112
  61.6 9.5 %collective-permute-start.6 = (f32[128,1152]{1,0:T(8,128)S(1)}, f32[128,1152]{1,0:T(8,128)S(1)}, u32[]{:S(2)}, u32[]{:S(2)}) collective-permute-start(f32[128,1152]{1,0:T(8,128)S(1)} %get-tuple-element.57), channel_id=1, source_target_pairs={{0,2},{1,511},{2,4},{3,1},{4,6},{5,3},{6,8},{7,5},{8,10},{9,7},{10... | collective-permute-start | bytes 1769480 | tf_op jit(solution)/shard_map/ppermute | solution.py:141
  71.2 0.0 collective-permute-done.5.hat
  71.2 1.9 %far_image.1.tgrad = f32[256,1152]{1,0:T(8,128)S(1)} custom-call(f32[1]{0:T(128)S(6)} %copy.6.scale, f32[1]{0:T(128)S(6)} %copy.7.bias, bf16[256,1152]{1,0:T(8,128)(2,1)S(1)} %get-tuple-element.33.thi.hi, bf16[256,1152]{1,0:T(8,128)(2,1)S(1)} %get-tuple-element.34.tlo.lo, f32[128,1152]{1,0:T(8,128)S(1)} %collective-permute-done.5.hat, ...), custom_call_target="tpu_custom_call" | custom-call | flops 99999997952 | tf_op jit(solution)/shard_map/far_image/pallas_call | solution.py:112
  73.1 0.0 collective-permute-done.3.stack
  73.1 4.5 %cross_tiles.1 = (f32[256,1152]{1,0:T(8,128)}, f32[256,1152]{1,0:T(8,128)S(1)}) custom-call(f32[1]{0:T(128)S(6)} %copy.6.scale, f32[1]{0:T(128)S(6)} %copy.7.bias, bf16[256,1152]{1,0:T(8,128)(2,1)S(1)} %get-tuple-element.31.hi.ihi, bf16[256,1152]{1,0:T(8,128)(2,1)S(1)} %get-tuple-element.32.lo.ilo, bf16[256,1152]{1,0:T(8,128)(2,1)S(1)} %get-tuple-element.33.thi.hi, ...), custom_call_target="tpu_custom_call" | custom-call | flops 1 | tf_op jit(solution)/shard_map/cross_tiles/pallas_call | solution.py:112
  77.6 0.4 collective-permute-done.6.hat
  78.0 3.0 %last_image.1 = f32[256,1152]{1,0:T(8,128)} custom-call(f32[1]{0:T(128)S(6)} %copy.6.scale, f32[1]{0:T(128)S(6)} %copy.7.bias, bf16[256,1152]{1,0:T(8,128)(2,1)S(1)} %get-tuple-element.33.thi.hi, bf16[256,1152]{1,0:T(8,128)(2,1)S(1)} %get-tuple-element.34.tlo.lo, f32[128,1152]{1,0:T(8,128)S(1)} %collective-permute-done.6.hat, ...), custom_call_target="tpu_custom_call" | custom-call | flops 1 | tf_op jit(solution)/shard_map/last_image/pallas_call | solution.py:112
Async XLA Ops:
  0.6 33.1 %collective-permute-start.1 = (f32[256,1152]{1,0:T(8,128)}, f32[256,1152]{1,0:T(8,128)S(1)}, u32[]{:S(2)}, u32[]{:S(2)}) collective-permute-start(f32[256,1152]{1,0:T(8,128)} %txt.1), channel_id=1, source_target_pairs={{0,510},{1,3},{2,0},{3,5},{4,2},{5,7},{6,4},{7,9},{8,6},{9,11},{10... | collective-permute-start | bytes 3538952 | tf_op jit(solution)/shard_map/ppermute | solution.py:136
  5.9 1.3 %copy-start = (f32[256,1152]{1,0:T(8,128)S(1)}, f32[256,1152]{1,0:T(8,128)}, u32[]{:S(2)}) copy-start(f32[256,1152]{1,0:T(8,128)} %img.1) | copy-start | bytes 3538948
  7.1 1.3 %copy-start.1 = (f32[256,1152]{1,0:T(8,128)S(1)}, f32[256,1152]{1,0:T(8,128)}, u32[]{:S(2)}) copy-start(f32[256,1152]{1,0:T(8,128)} %txt.1) | copy-start | bytes 3538948
  13.3 32.5 %collective-permute-start = (f32[256,1152]{1,0:T(8,128)S(1)}, f32[256,1152]{1,0:T(8,128)S(1)}, u32[]{:S(2)}, u32[]{:S(2)}) collective-permute-start(f32[256,1152]{1,0:T(8,128)S(1)} %get-tuple-element.35), channel_id=1, source_target_pairs={{0,510},{1,3},{2,0},{3,5},{4,2},{5,7},{6,4},{7,9},{8,6},{9,11},{10... | collective-permute-start | bytes 3538952 | tf_op jit(solution)/shard_map/ppermute | solution.py:136
  16.4 21.9 %collective-permute-start.2 = (f32[512,1152]{1,0:T(8,128)S(1)}, f32[512,1152]{1,0:T(8,128)S(1)}, u32[]{:S(2)}, u32[]{:S(2)}) collective-permute-start(f32[512,1152]{1,0:T(8,128)S(1)} %get-tuple-element.38.own), channel_id=1, source_target_pairs={{0,1},{1,0},{2,3},{3,2},{4,5},{5,4},{6,7},{7,6},{8,9},{9,8},{10,11... | collective-permute-start | bytes 7077896 | tf_op jit(solution)/shard_map/ppermute | solution.py:146
  31.5 27.8 %collective-permute-start.4 = (f32[256,1152]{1,0:T(8,128)S(1)}, f32[256,1152]{1,0:T(8,128)S(1)}, u32[]{:S(2)}, u32[]{:S(2)}) collective-permute-start(f32[256,1152]{1,0:T(8,128)S(1)} %get-tuple-element.45.own), channel_id=1, source_target_pairs={{0,2},{1,511},{2,4},{3,1},{4,6},{5,3},{6,8},{7,5},{8,10},{9,7},{10... | collective-permute-start | bytes 3538952 | tf_op jit(solution)/shard_map/ppermute | solution.py:141
  36.2 35.0 %collective-permute-start.5 = (f32[128,1152]{1,0:T(8,128)S(1)}, f32[128,1152]{1,0:T(8,128)S(1)}, u32[]{:S(2)}, u32[]{:S(2)}) collective-permute-start(f32[128,1152]{1,0:T(8,128)S(1)} %get-tuple-element.53), channel_id=1, source_target_pairs={{0,2},{1,511},{2,4},{3,1},{4,6},{5,3},{6,8},{7,5},{8,10},{9,7},{10... | collective-permute-start | bytes 1769480 | tf_op jit(solution)/shard_map/ppermute | solution.py:141
  48.2 24.8 %collective-permute-start.3 = (f32[512,1152]{1,0:T(8,128)S(1)}, f32[512,1152]{1,0:T(8,128)S(1)}, u32[]{:S(2)}, u32[]{:S(2)}) collective-permute-start(f32[512,1152]{1,0:T(8,128)S(1)} %get-tuple-element.44), channel_id=1, source_target_pairs={{0,1},{1,0},{2,3},{3,2},{4,5},{5,4},{6,7},{7,6},{8,9},{9,8},{10,11... | collective-permute-start | bytes 7077896 | tf_op jit(solution)/shard_map/ppermute | solution.py:146
  61.6 16.4 %collective-permute-start.6 = (f32[128,1152]{1,0:T(8,128)S(1)}, f32[128,1152]{1,0:T(8,128)S(1)}, u32[]{:S(2)}, u32[]{:S(2)}) collective-permute-start(f32[128,1152]{1,0:T(8,128)S(1)} %get-tuple-element.57), channel_id=1, source_target_pairs={{0,2},{1,511},{2,4},{3,1},{4,6},{5,3},{6,8},{7,5},{8,10},{9,7},{10... | collective-permute-start | bytes 1769480 | tf_op jit(solution)/shard_map/ppermute | solution.py:141

commit v2 on v1

v2 whole, which is shorter than its diff:
```python
import functools

import jax
import jax.numpy as jnp
from jax import lax
from jax.experimental import pallas as pl
from jax.experimental.pallas import tpu as pltpu
from jax.sharding import PartitionSpec as P

F32 = jnp.float32
BF16 = jnp.bfloat16
VMEM = pl.BlockSpec(memory_space=pltpu.VMEM)
SMEM = pl.BlockSpec(memory_space=pltpu.SMEM)
HBM = pl.BlockSpec(memory_space=pltpu.HBM)
PARTS = 4
COLUMNS = 256
NT = (((1,), (1,)), ((), ()))
NN = (((1,), (0,)), ((), ()))


def split(value):
    hi = value.astype(BF16)
    return hi, (value - hi.astype(F32)).astype(BF16)


def product(left, right, dims):
    mul = functools.partial(
        lax.dot_general, dimension_numbers=dims, preferred_element_type=F32
    )
    (lh, ll), (rh, rl) = left, right
    return mul(lh, rh) + (mul(lh, rl) + mul(ll, rh))


def unit(raw):
    inv = 1.0 / jnp.sqrt(jnp.sum(raw * raw, axis=1, keepdims=True) + 1e-06)
    return raw * inv, inv


def tile_grad(x, y, scale, bias, matching=False):
    logits = scale * product(x, y, NT) + bias
    if matching:
        diag = lax.broadcasted_iota(jnp.int32, logits.shape, 0) == (
            lax.broadcasted_iota(jnp.int32, logits.shape, 1)
        )
        sign = jnp.where(diag, -1.0, 1.0)
        coeff = sign * jax.nn.sigmoid(sign * logits)
    else:
        coeff = jax.nn.sigmoid(logits)
    return product(split(coeff), y, NN)


def unit_kernel(img_in, txt_in, ihat, that, both, *refs):
    (iinv, ihi, ilo, tinv, thi, tlo, raw, sems) = refs
    rows = ihat.shape[0]
    part = rows // PARTS
    copies = []
    for n, source in enumerate((img_in, txt_in)):
        for k in range(PARTS):
            copies.append(
                pltpu.make_async_copy(
                    source.at[pl.ds(k * part, part)],
                    raw.at[pl.ds(n * rows + k * part, part)],
                    sems.at[n, k],
                )
            )
    for copy in copies:
        copy.start()
    for n, (hat, inv, hi, lo) in enumerate(((ihat, iinv, ihi, ilo), (that, tinv, thi, tlo))):
        for copy in copies[n * PARTS : (n + 1) * PARTS]:
            copy.wait()
        hat[...], inv[...] = unit(raw[n * rows : (n + 1) * rows])
        both[n * rows : (n + 1) * rows] = hat[...]
        hi[...], lo[...] = split(hat[...])


def own_kernel(scale, bias, ihi, ilo, thi, tlo, igrad, tgrad):
    x, y = (ihi[...], ilo[...]), (thi[...], tlo[...])
    igrad[...] = tile_grad(x, y, scale[0], bias[0], True)
    tgrad[...] = tile_grad(y, x, scale[0], bias[0], True)


def tile_kernel(scale, bias, hi, lo, hat, grad, total):
    total[...] = grad[...] + tile_grad(
        (hi[...], lo[...]), split(hat[...]), scale[0], bias[0]
    )


def raw_kernel(scale, bias, hi, lo, raw, grad, hat, total):
    hat[...] = unit(raw[...])[0]
    tile_kernel(scale, bias, hi, lo, hat, grad, total)


def pair_kernel(scale, bias, ihi, ilo, thi, tlo, both, igrad, tgrad, itotal, ttotal):
    rows = igrad.shape[0]
    tile_kernel(scale, bias, ihi, ilo, both.at[rows:], igrad, itotal)
    tile_kernel(scale, bias, thi, tlo, both.at[:rows], tgrad, ttotal)


def cross_kernel(scale, bias, hi, lo, hat, grad, own, total, inner):
    tile_kernel(scale, bias, hi, lo, hat, grad, total)
    inner[...] = jnp.sum(own[...] * total[...], axis=1, keepdims=True)


def last_kernel(scale, bias, hi, lo, hat, grad, own, inner, inv, out, part, sems):
    y = split(hat[...])
    dots = product((hi[...], lo[...]), y, NT)
    coeff = jax.nn.sigmoid(scale[0] * dots + bias[0])
    along = inner[...] + jnp.sum(coeff * dots, axis=1, keepdims=True)
    factor = scale[0] * inv[...]
    coeff = split(coeff)
    copies = []
    width = hat.shape[1]
    for at in range(0, width, COLUMNS):
        here = slice(at, min(at + COLUMNS, width))
        total = grad[:, here] + product(coeff, [half[:, here] for half in y], NN)
        part[:, here] = (total - own[:, here] * along) * factor
        wide = pl.ds(at, here.stop - at)
        copies.append(
            pltpu.make_async_copy(
                part.at[:, wide], out.at[:, wide], sems.at[at // COLUMNS]
            )
        )
        copies[-1].start()
    for copy in copies:
        copy.wait()


def call(kernel, name, operands, outs, scalars=2, spec=VMEM, out_spec=VMEM, **extra):
    return pl.pallas_call(
        kernel,
        name=name,
        out_shape=outs,
        in_specs=[SMEM] * scalars + [spec] * (len(operands) - scalars),
        out_specs=jax.tree.map(lambda _: out_spec, outs),
        compiler_params=pltpu.CompilerParams(vmem_limit_bytes=24 * 2**20),
        cost_estimate=pl.CostEstimate(flops=2 * 10**10, bytes_accessed=0, transcendentals=0),
        **extra,
    )(*operands)


def body(image_embed, text_embed, logit_scale, logit_bias):
    rows, width = image_embed.shape
    size = lax.axis_size("dp")

    def shape(height, wide=width, kind=F32):
        return jax.ShapeDtypeStruct((height, wide), kind)

    one = shape(rows)
    column = shape(rows, 1)
    state = (column, shape(rows, kind=BF16), shape(rows, kind=BF16))
    tb = (logit_scale, logit_bias)

    def outward(block):
        return lax.ppermute(
            block, "dp", [(d, (d + (2 if d % 2 else -2)) % size) for d in range(size)]
        )

    def inward(block):
        return lax.ppermute(
            block, "dp", [(d, (d + (-2 if d % 2 else 2)) % size) for d in range(size)]
        )

    def swap(block):
        return lax.ppermute(block, "dp", [(d, d ^ 1) for d in range(size)])

    def last(name, *operands):
        return call(
            last_kernel,
            name,
            (*tb, *operands),
            one,
            out_spec=HBM,
            scratch_shapes=[
                pltpu.VMEM((rows, width), F32),
                pltpu.SemaphoreType.DMA((pl.cdiv(width, COLUMNS),)),
            ],
        )

    def after(*values):
        return lax.optimization_barrier(values)

    near_txt = outward(text_embed)
    in_hbm = [
        pltpu.with_memory_space_constraint(raw, pltpu.HBM)
        for raw in (image_embed, text_embed)
    ]
    ihat, that, both, *rest = call(
        unit_kernel,
        "unit_rows",
        in_hbm,
        (one, one, shape(2 * rows), *state, *state),
        scalars=0,
        spec=HBM,
        scratch_shapes=[
            pltpu.VMEM((2 * rows, width), F32),
            pltpu.SemaphoreType.DMA((2, PARTS)),
        ],
    )
    iinv, ihi, ilo, tinv, thi, tlo = rest
    img, txt = (ihi, ilo), (thi, tlo)
    near_img = outward(ihat)
    pair = swap(both)
    igrad, tgrad = call(own_kernel, "own_tiles", (*tb, *img, *txt), (one, one))

    that_late, igrad, tgrad = after(that, igrad, tgrad)
    far_txt = inward(that_late)
    near_txt, igrad = call(
        raw_kernel, "near_text", (*tb, *img, near_txt, igrad), (one, one)
    )
    ihat_late, near_txt, igrad = after(ihat, near_txt, igrad)
    far_img = inward(ihat_late)
    cross_txt = swap(near_txt)
    igrad, tgrad = call(
        pair_kernel, "pair_tiles", (*tb, *img, *txt, pair, igrad, tgrad), (one, one)
    )
    igrad, inner_img = call(
        cross_kernel, "cross_text", (*tb, *img, cross_txt, igrad, ihat), (one, column)
    )

    near_img, igrad = after(near_img, igrad)
    cross_img = swap(near_img)
    tgrad = call(tile_kernel, "near_image", (*tb, *txt, near_img, tgrad), one)

    far_txt, igrad, tgrad = after(far_txt, igrad, tgrad)
    grad_image = last("last_text", *img, far_txt, igrad, ihat, inner_img, iinv)
    cross_img, grad_image = after(cross_img, grad_image)
    tgrad, inner_txt = call(
        cross_kernel, "cross_image", (*tb, *txt, cross_img, tgrad, that), (one, column)
    )
    grad_text = last("last_image", *txt, far_img, tgrad, that, inner_txt, tinv)
    return grad_image, grad_text


def solution(mesh):
    return jax.shard_map(
        body,
        mesh=mesh,
        in_specs=(P("dp", None), P("dp", None), P(), P()),
        out_specs=(P("dp", None), P("dp", None)),
        check_vma=False,
    )
```

time: 81.4 us -> 73.1 us (0.90)
  starting transfers between devices: 47.2 us -> 37.2 us
  waiting for transfers between devices: 3.54 us -> 7.11 us
  local copies, waits for them, and re-layouts: 2.53 us -> 0 us
    ppermute x2 -> x3, starting transfers between devices: 26.2 us -> 19.5 us  [swap(): return lax.ppermute(block, 'dp', [(d, d ^ 1) for d in range(size)])]
    ppermute x3 -> x2, waiting for transfers between devices: 0.44 us -> 7.1 us  [inward(): lax.ppermute(block, 'dp', [(d, (d + (-2 if d % 2 else 2)) % size) for d i...]
    ppermute x2, waiting for transfers between devices: 3.1 us -> 0.01 us  [outward(): lax.ppermute(block, 'dp', [(d, (d + (2 if d % 2 else -2)) % size) for d i...]
    unnamed x4 -> x0, local copies, waits for them, and re-layouts: 2.53 us -> none
    ppermute x3 -> x2, starting transfers between devices: 13.9 us -> 11.8 us  [inward(): lax.ppermute(block, 'dp', [(d, (d + (-2 if d % 2 else 2)) % size) for d i...]
    ppermute x2, starting transfers between devices: 7.07 us -> 5.87 us  [outward(): lax.ppermute(block, 'dp', [(d, (d + (2 if d % 2 else -2)) % size) for d i...]
    pallas_call x8 -> x9, Pallas kernels: 25.7 us -> 26.2 us  [call(): pl.pallas_call(kernel, name=name, out_shape=outs, in_specs=[SMEM] * scala...]
  transfers between devices with their start and end apart: 7 -> 7, of which waited for: 2 -> 1; matrix products, arithmetic and copies ran while one was open for 0% -> 0% of each run, Pallas kernels for 28% -> 32%
where the time goes in v2:
time: 73.1 us; the launch traced here: 72.8 us
  starting transfers between devices  37.2 us (51%)
  Pallas kernels  26.2 us (36%)
  waiting for transfers between devices  7.11 us (10%)
  between operations  2.22 us (3%)
    pallas_call x9, Pallas kernels, call(): pl.pallas_call(kernel, name=name, out_shape=outs, in_specs=[SMEM] * scala...  26.2 us
    ppermute x3, starting transfers between devices, swap(): return lax.ppermute(block, 'dp', [(d, d ^ 1) for d in range(size)])  19.5 us
    ppermute x2, starting transfers between devices, inward(): lax.ppermute(block, 'dp', [(d, (d + (-2 if d % 2 else 2)) % size) for d i...  11.8 us
    ppermute x2, waiting for transfers between devices, inward(): lax.ppermute(block, 'dp', [(d, (d + (-2 if d % 2 else 2)) % size) for d i...  7.1 us
    ppermute x2, starting transfers between devices, outward(): lax.ppermute(block, 'dp', [(d, (d + (2 if d % 2 else -2)) % size) for d i...  5.87 us
  transfers between devices with their start and end apart: 7, of which 1 were waited for; matrix products, arithmetic and copies ran while one was open for 0% of the time, Pallas kernels for 32%

profile of v2, /device:TPU:1, one launch (start us, length us, event | category | flops | bytes accessed | tf_op | source)
XLA Modules:
  0.0 72.8 jit_solution(14790114267725517766)
XLA Ops:
  0.6 3.9 %collective-permute-start.1 = (f32[256,1152]{1,0:T(8,128)}, f32[256,1152]{1,0:T(8,128)S(1)}, u32[]{:S(2)}, u32[]{:S(2)}) collective-permute-start(f32[256,1152]{1,0:T(8,128)} %txt_in.1), channel_id=1, source_target_pairs={{0,510},{1,3},{2,0},{3,5},{4,2},{5,7},{6,4},{7,9},{8,6},{9,11},{10... | collective-permute-start | bytes 3538952 | tf_op jit(solution)/shard_map/ppermute | solution.py:154
  4.6 2.1 %unit_rows.1 = (f32[256,1152]{1,0:T(8,128)S(1)}, f32[256,1152]{1,0:T(8,128)S(1)}, f32[512,1152]{1,0:T(8,128)S(1)}, f32[256,1]{1,0:T(8,128)S(1)}, bf16[256,1152]{...) custom-call(f32[256,1152]{1,0:T(8,128)} %img_in.1, ...), custom_call_target="tpu_custom_call" | custom-call | flops 20000000000 | tf_op jit(solution)/shard_map/unit_rows/pallas_call | solution.py:129
  6.6 15.5 %collective-permute-start.3 = (f32[512,1152]{1,0:T(8,128)S(1)}, f32[512,1152]{1,0:T(8,128)S(1)}, u32[]{:S(2)}, u32[]{:S(2)}) collective-permute-start(f32[512,1152]{1,0:T(8,128)S(1)} %get-tuple-element.46), channel_id=1, source_target_pairs={{0,1},{1,0},{2,3},{3,2},{4,5},{5,4},{6,7},{7,6},{8,9},{9,8},{10,11... | collective-permute-start | bytes 7077896 | tf_op jit(solution)/shard_map/ppermute | solution.py:164
  22.2 1.9 %collective-permute-start = (f32[256,1152]{1,0:T(8,128)S(1)}, f32[256,1152]{1,0:T(8,128)S(1)}, u32[]{:S(2)}, u32[]{:S(2)}) collective-permute-start(f32[256,1152]{1,0:T(8,128)S(1)} %get-tuple-element.60.own), channel_id=1, source_target_pairs={{0,510},{1,3},{2,0},{3,5},{4,2},{5,7},{6,4},{7,9},{8,6},{9,11},{10... | collective-permute-start | bytes 3538952 | tf_op jit(solution)/shard_map/ppermute | solution.py:154
  25.4 4.4 %own_tiles.1 = (f32[256,1152]{1,0:T(8,128)S(1)}, f32[256,1152]{1,0:T(8,128)S(1)}) custom-call(f32[1]{0:T(128)S(6)} %copy.6.scale, f32[1]{0:T(128)S(6)} %copy.7.bias, bf16[256,1152]{1,0:T(8,128)(2,1)S(1)} %get-tuple-element.35.ihi.hi, bf16[256,1152]{1,0:T(8,128)(2,1)S(1)} %get-tuple-element.36.ilo.lo, bf16[256,1152]{1,0:T(8,128)(2,1)S(1)} %get-tuple-element.38.thi.hi, ...), custom_call_target="tpu_custom_call" | custom-call | flops 20000000000 | tf_op jit(solution)/shard_map/own_tiles/pallas_call | solution.py:129
  29.8 8.8 %collective-permute-start.5 = (f32[256,1152]{1,0:T(8,128)S(1)}, f32[256,1152]{1,0:T(8,128)S(1)}, u32[]{:S(2)}, u32[]{:S(2)}) collective-permute-start(f32[256,1152]{1,0:T(8,128)S(1)} %get-tuple-element.52.own), channel_id=1, source_target_pairs={{0,2},{1,511},{2,4},{3,1},{4,6},{5,3},{6,8},{7,5},{8,10},{9,7},{10... | collective-permute-start | bytes 3538952 | tf_op jit(solution)/shard_map/ppermute | solution.py:159
  38.6 0.0 collective-permute-done.1.raw
  38.6 2.4 %near_text.1 = (f32[256,1152]{1,0:T(8,128)S(1)}, f32[256,1152]{1,0:T(8,128)S(1)}) custom-call(f32[1]{0:T(128)S(6)} %copy.6.scale, f32[1]{0:T(128)S(6)} %copy.7.bias, bf16[256,1152]{1,0:T(8,128)(2,1)S(1)} %get-tuple-element.35.ihi.hi, bf16[256,1152]{1,0:T(8,128)(2,1)S(1)} %get-tuple-element.36.ilo.lo, f32[256,1152]{1,0:T(8,128)S(1)} %collective-permute-done.1.raw, ...), custom_call_target="tpu_custom_call" | custom-call | flops 20000000000 | tf_op jit(solution)/shard_map/near_text/pallas_call | solution.py:129
  41.0 1.9 %collective-permute-start.2 = (f32[256,1152]{1,0:T(8,128)S(1)}, f32[256,1152]{1,0:T(8,128)S(1)}, u32[]{:S(2)}, u32[]{:S(2)}) collective-permute-start(f32[256,1152]{1,0:T(8,128)S(1)} %get-tuple-element.45), channel_id=1, source_target_pairs={{0,1},{1,0},{2,3},{3,2},{4,5},{5,4},{6,7},{7,6},{8,9},{9,8},{10,11... | collective-permute-start | bytes 3538952 | tf_op jit(solution)/shard_map/ppermute | solution.py:164
  42.9 3.0 %collective-permute-start.6 = (f32[256,1152]{1,0:T(8,128)S(1)}, f32[256,1152]{1,0:T(8,128)S(1)}, u32[]{:S(2)}, u32[]{:S(2)}) collective-permute-start(f32[256,1152]{1,0:T(8,128)S(1)} %get-tuple-element.60.own), channel_id=1, source_target_pairs={{0,2},{1,511},{2,4},{3,1},{4,6},{5,3},{6,8},{7,5},{8,10},{9,7},{10... | collective-permute-start | bytes 3538952 | tf_op jit(solution)/shard_map/ppermute | solution.py:159
  46.0 0.0 collective-permute-done.3.both
  46.0 4.4 %pair_tiles.1 = (f32[256,1152]{1,0:T(8,128)S(1)}, f32[256,1152]{1,0:T(8,128)S(1)}) custom-call(f32[1]{0:T(128)S(6)} %copy.6.scale, f32[1]{0:T(128)S(6)} %copy.7.bias, bf16[256,1152]{1,0:T(8,128)(2,1)S(1)} %get-tuple-element.35.ihi.hi, bf16[256,1152]{1,0:T(8,128)(2,1)S(1)} %get-tuple-element.36.ilo.lo, bf16[256,1152]{1,0:T(8,128)(2,1)S(1)} %get-tuple-element.38.thi.hi, ...), custom_call_target="tpu_custom_call" | custom-call | flops 20000000000 | tf_op jit(solution)/shard_map/pair_tiles/pallas_call | solution.py:129
  50.4 0.0 collective-permute-done.2.hat
  50.4 2.4 %cross_text.1 = (f32[256,1152]{1,0:T(8,128)S(1)}, f32[256,1]{1,0:T(8,128)S(1)}) custom-call(f32[1]{0:T(128)S(6)} %copy.6.scale, f32[1]{0:T(128)S(6)} %copy.7.bias, bf16[256,1152]{1,0:T(8,128)(2,1)S(1)} %get-tuple-element.35.ihi.hi, bf16[256,1152]{1,0:T(8,128)(2,1)S(1)} %get-tuple-element.36.ilo.lo, f32[256,1152]{1,0:T(8,128)S(1)} %collective-permute-done.2.hat, ...), custom_call_target="tpu_custom_call" | custom-call | flops 20000000000 | tf_op jit(solution)/shard_map/cross_text/pallas_call | solution.py:129
  52.7 0.0 collective-permute-done.hat
  52.7 2.1 %collective-permute-start.4 = (f32[256,1152]{1,0:T(8,128)S(1)}, f32[256,1152]{1,0:T(8,128)S(1)}, u32[]{:S(2)}, u32[]{:S(2)}) collective-permute-start(f32[256,1152]{1,0:T(8,128)S(1)} %collective-permute-done.hat), channel_id=1, source_target_pairs={{0,1},{1,0},{2,3},{3,2},{4,5},{5,4},{6,7},{7,6},{8,9},{9,8},{10,11... | collective-permute-start | bytes 3538952 | tf_op jit(solution)/shard_map/ppermute | solution.py:164
  54.9 2.3 %near_image.1.grad = f32[256,1152]{1,0:T(8,128)S(1)} custom-call(f32[1]{0:T(128)S(6)} %copy.6.scale, f32[1]{0:T(128)S(6)} %copy.7.bias, bf16[256,1152]{1,0:T(8,128)(2,1)S(1)} %get-tuple-element.38.thi.hi, bf16[256,1152]{1,0:T(8,128)(2,1)S(1)} %get-tuple-element.39.tlo.lo, f32[256,1152]{1,0:T(8,128)S(1)} %collective-permute-done.hat, ...), custom_call_target="tpu_custom_call" | custom-call | flops 20000000000 | tf_op jit(solution)/shard_map/near_image/pallas_call | solution.py:129
  57.1 0.0 collective-permute-done.5.hat
  57.2 3.0 %last_text.1 = f32[256,1152]{1,0:T(8,128)} custom-call(f32[1]{0:T(128)S(6)} %copy.6.scale, f32[1]{0:T(128)S(6)} %copy.7.bias, bf16[256,1152]{1,0:T(8,128)(2,1)S(1)} %get-tuple-element.35.ihi.hi, bf16[256,1152]{1,0:T(8,128)(2,1)S(1)} %get-tuple-element.36.ilo.lo, f32[256,1152]{1,0:T(8,128)S(1)} %collective-permute-done.5.hat, ...), custom_call_target="tpu_custom_call" | custom-call | flops 20000000000 | tf_op jit(solution)/shard_map/last_text/pallas_call | solution.py:129
  60.1 0.0 collective-permute-done.4.hat
  60.2 2.4 %cross_image.1 = (f32[256,1152]{1,0:T(8,128)S(1)}, f32[256,1]{1,0:T(8,128)S(1)}) custom-call(f32[1]{0:T(128)S(6)} %copy.6.scale, f32[1]{0:T(128)S(6)} %copy.7.bias, bf16[256,1152]{1,0:T(8,128)(2,1)S(1)} %get-tuple-element.38.thi.hi, bf16[256,1152]{1,0:T(8,128)(2,1)S(1)} %get-tuple-element.39.tlo.lo, f32[256,1152]{1,0:T(8,128)S(1)} %collective-permute-done.4.hat, ...), custom_call_target="tpu_custom_call" | custom-call | flops 20000000000 | tf_op jit(solution)/shard_map/cross_image/pallas_call | solution.py:129
  62.5 7.1 %collective-permute-done.6.hat = f32[256,1152]{1,0:T(8,128)S(1)} collective-permute-done((f32[256,1152]{1,0:T(8,128)S(1)}, f32[256,1152]{1,0:T(8,128)S(1)}, u32[]{:S(2)}, u32[]{:S(2)}) %collective-permute-start.6) | collective-permute-done | bytes 1179680 | tf_op jit(solution)/shard_map/ppermute | solution.py:159
  69.6 3.0 %last_image.1 = f32[256,1152]{1,0:T(8,128)} custom-call(f32[1]{0:T(128)S(6)} %copy.6.scale, f32[1]{0:T(128)S(6)} %copy.7.bias, bf16[256,1152]{1,0:T(8,128)(2,1)S(1)} %get-tuple-element.38.thi.hi, bf16[256,1152]{1,0:T(8,128)(2,1)S(1)} %get-tuple-element.39.tlo.lo, f32[256,1152]{1,0:T(8,128)S(1)} %collective-permute-done.6.hat, ...), custom_call_target="tpu_custom_call" | custom-call | flops 20000000000 | tf_op jit(solution)/shard_map/last_image/pallas_call | solution.py:129
Async XLA Ops:
  0.6 37.9 %collective-permute-start.1 = (f32[256,1152]{1,0:T(8,128)}, f32[256,1152]{1,0:T(8,128)S(1)}, u32[]{:S(2)}, u32[]{:S(2)}) collective-permute-start(f32[256,1152]{1,0:T(8,128)} %txt_in.1), channel_id=1, source_target_pairs={{0,510},{1,3},{2,0},{3,5},{4,2},{5,7},{6,4},{7,9},{8,6},{9,11},{10... | collective-permute-start | bytes 3538952 | tf_op jit(solution)/shard_map/ppermute | solution.py:154
  6.6 39.3 %collective-permute-start.3 = (f32[512,1152]{1,0:T(8,128)S(1)}, f32[512,1152]{1,0:T(8,128)S(1)}, u32[]{:S(2)}, u32[]{:S(2)}) collective-permute-start(f32[512,1152]{1,0:T(8,128)S(1)} %get-tuple-element.46), channel_id=1, source_target_pairs={{0,1},{1,0},{2,3},{3,2},{4,5},{5,4},{6,7},{7,6},{8,9},{9,8},{10,11... | collective-permute-start | bytes 7077896 | tf_op jit(solution)/shard_map/ppermute | solution.py:164
  22.2 30.6 %collective-permute-start = (f32[256,1152]{1,0:T(8,128)S(1)}, f32[256,1152]{1,0:T(8,128)S(1)}, u32[]{:S(2)}, u32[]{:S(2)}) collective-permute-start(f32[256,1152]{1,0:T(8,128)S(1)} %get-tuple-element.60.own), channel_id=1, source_target_pairs={{0,510},{1,3},{2,0},{3,5},{4,2},{5,7},{6,4},{7,9},{8,6},{9,11},{10... | collective-permute-start | bytes 3538952 | tf_op jit(solution)/shard_map/ppermute | solution.py:154
  29.8 27.4 %collective-permute-start.5 = (f32[256,1152]{1,0:T(8,128)S(1)}, f32[256,1152]{1,0:T(8,128)S(1)}, u32[]{:S(2)}, u32[]{:S(2)}) collective-permute-start(f32[256,1152]{1,0:T(8,128)S(1)} %get-tuple-element.52.own), channel_id=1, source_target_pairs={{0,2},{1,511},{2,4},{3,1},{4,6},{5,3},{6,8},{7,5},{8,10},{9,7},{10... | collective-permute-start | bytes 3538952 | tf_op jit(solution)/shard_map/ppermute | solution.py:159
  41.0 9.4 %collective-permute-start.2 = (f32[256,1152]{1,0:T(8,128)S(1)}, f32[256,1152]{1,0:T(8,128)S(1)}, u32[]{:S(2)}, u32[]{:S(2)}) collective-permute-start(f32[256,1152]{1,0:T(8,128)S(1)} %get-tuple-element.45), channel_id=1, source_target_pairs={{0,1},{1,0},{2,3},{3,2},{4,5},{5,4},{6,7},{7,6},{8,9},{9,8},{10,11... | collective-permute-start | bytes 3538952 | tf_op jit(solution)/shard_map/ppermute | solution.py:164
  42.9 26.7 %collective-permute-start.6 = (f32[256,1152]{1,0:T(8,128)S(1)}, f32[256,1152]{1,0:T(8,128)S(1)}, u32[]{:S(2)}, u32[]{:S(2)}) collective-permute-start(f32[256,1152]{1,0:T(8,128)S(1)} %get-tuple-element.60.own), channel_id=1, source_target_pairs={{0,2},{1,511},{2,4},{3,1},{4,6},{5,3},{6,8},{7,5},{8,10},{9,7},{10... | collective-permute-start | bytes 3538952 | tf_op jit(solution)/shard_map/ppermute | solution.py:159
  52.7 7.4 %collective-permute-start.4 = (f32[256,1152]{1,0:T(8,128)S(1)}, f32[256,1152]{1,0:T(8,128)S(1)}, u32[]{:S(2)}, u32[]{:S(2)}) collective-permute-start(f32[256,1152]{1,0:T(8,128)S(1)} %collective-permute-done.hat), channel_id=1, source_target_pairs={{0,1},{1,0},{2,3},{3,2},{4,5},{5,4},{6,7},{7,6},{8,9},{9,8},{10,11... | collective-permute-start | bytes 3538952 | tf_op jit(solution)/shard_map/ppermute | solution.py:164

commit v3 on v2

--- a/solution.py
+++ b/solution.py
@@ -14,6 +14,8 @@
 HBM = pl.BlockSpec(memory_space=pltpu.HBM)
 PARTS = 4
 COLUMNS = 256
+SEAM = 128
+LATE = ("last_text", "cross_image", "far_image")
 NT = (((1,), (1,)), ((), ()))
 NN = (((1,), (0,)), ((), ()))
 
@@ -49,7 +51,7 @@
     return product(split(coeff), y, NN)
 
 
-def unit_kernel(img_in, txt_in, ihat, that, both, *refs):
+def unit_kernel(img_in, txt_in, ihat, that, both, ihat_a, ihat_b, *refs):
     (iinv, ihi, ilo, tinv, thi, tlo, raw, sems) = refs
     rows = ihat.shape[0]
     part = rows // PARTS
@@ -71,6 +73,9 @@
         hat[...], inv[...] = unit(raw[n * rows : (n + 1) * rows])
         both[n * rows : (n + 1) * rows] = hat[...]
         hi[...], lo[...] = split(hat[...])
+        if n == 0:
+            ihat_a[...] = hat[: ihat_a.shape[0]]
+            ihat_b[...] = hat[ihat_a.shape[0] :]
 
 
 def own_kernel(scale, bias, ihi, ilo, thi, tlo, igrad, tgrad):
@@ -101,18 +106,40 @@
     inner[...] = jnp.sum(own[...] * total[...], axis=1, keepdims=True)
 
 
-def last_kernel(scale, bias, hi, lo, hat, grad, own, inner, inv, out, part, sems):
-    y = split(hat[...])
-    dots = product((hi[...], lo[...]), y, NT)
-    coeff = jax.nn.sigmoid(scale[0] * dots + bias[0])
+def stacked(hi, lo, y_hi, y_lo, scale, bias):
+    rows = y_hi.shape[0]
+    mul = functools.partial(lax.dot_general, preferred_element_type=F32)
+    both = mul(hi, jnp.concatenate([y_hi, y_lo], axis=0), NT)
+    dots = both[:, :rows] + (both[:, rows:] + mul(lo, y_hi, NT))
+    coeff = jax.nn.sigmoid(scale * dots + bias)
+    top, rest = split(coeff)
+    left = jnp.concatenate([top, rest], axis=1)
+    right = jnp.concatenate([y_hi, y_hi], axis=0)
+    return dots, coeff, lambda here: (
+        mul(left, right[:, here], NN) + mul(top, y_lo[:, here], NN)
+    )
+
+
+def last_kernel(hats, scale, bias, hi, lo, *refs):
+    grad, own, inner, inv, out, part, sems = refs[hats:]
+    hat = refs[0][...]
+    for more in refs[1:hats]:
+        hat += more[...]
+    y = split(hat)
+    if 2 * hat.shape[0] <= hi.shape[0]:
+        dots, coeff, columns = stacked(hi[...], lo[...], *y, scale[0], bias[0])
+    else:
+        dots = product((hi[...], lo[...]), y, NT)
+        coeff = jax.nn.sigmoid(scale[0] * dots + bias[0])
+        halves = split(coeff)
+        columns = lambda here: product(halves, [half[:, here] for half in y], NN)
     along = inner[...] + jnp.sum(coeff * dots, axis=1, keepdims=True)
     factor = scale[0] * inv[...]
-    coeff = split(coeff)
     copies = []
     width = hat.shape[1]
     for at in range(0, width, COLUMNS):
         here = slice(at, min(at + COLUMNS, width))
-        total = grad[:, here] + product(coeff, [half[:, here] for half in y], NN)
+        total = grad[:, here] + columns(here)
         part[:, here] = (total - own[:, here] * along) * factor
         wide = pl.ds(at, here.stop - at)
         copies.append(
@@ -133,7 +160,9 @@
         in_specs=[SMEM] * scalars + [spec] * (len(operands) - scalars),
         out_specs=jax.tree.map(lambda _: out_spec, outs),
         compiler_params=pltpu.CompilerParams(vmem_limit_bytes=24 * 2**20),
-        cost_estimate=pl.CostEstimate(flops=2 * 10**10, bytes_accessed=0, transcendentals=0),
+        cost_estimate=pl.CostEstimate(
+            flops=1 if name in LATE else 2 * 10**10, bytes_accessed=0, transcendentals=0
+        ),
         **extra,
     )(*operands)
 
@@ -146,6 +175,7 @@
         return jax.ShapeDtypeStruct((height, wide), kind)
 
     one = shape(rows)
+    tail = rows // 2
     column = shape(rows, 1)
     state = (column, shape(rows, kind=BF16), shape(rows, kind=BF16))
     tb = (logit_scale, logit_bias)
@@ -155,17 +185,30 @@
             block, "dp", [(d, (d + (2 if d % 2 else -2)) % size) for d in range(size)]
         )
 
-    def inward(block):
-        return lax.ppermute(
-            block, "dp", [(d, (d + (-2 if d % 2 else 2)) % size) for d in range(size)]
-        )
+    def inward(block, skip=()):
+        pairs = [(d, (d + (-2 if d % 2 else 2)) % size) for d in range(size)]
+        return lax.ppermute(block, "dp", [pair for pair in pairs if pair not in skip])
+
+    seams = range(0, size, SEAM)
+    direct = [
+        pair
+        for at in seams
+        for pair in (((at - 2) % size, at), (at + 1, (at - 1) % size))
+    ]
+    via = [mid for at in seams for mid in ((at + 14) % size, (at - 15) % size)]
+
+    def relay_out(block):
+        return lax.ppermute(block, "dp", [(pair[0], mid) for pair, mid in zip(direct, via)])
+
+    def relay_in(block):
+        return lax.ppermute(block, "dp", [(mid, pair[1]) for pair, mid in zip(direct, via)])
 
     def swap(block):
         return lax.ppermute(block, "dp", [(d, d ^ 1) for d in range(size)])
 
-    def last(name, *operands):
+    def last(name, hats, *operands):
         return call(
-            last_kernel,
+            functools.partial(last_kernel, hats),
             name,
             (*tb, *operands),
             one,
@@ -184,11 +227,11 @@
         pltpu.with_memory_space_constraint(raw, pltpu.HBM)
         for raw in (image_embed, text_embed)
     ]
-    ihat, that, both, *rest = call(
+    ihat, that, both, ihat_a, ihat_b, *rest = call(
         unit_kernel,
         "unit_rows",
         in_hbm,
-        (one, one, shape(2 * rows), *state, *state),
+        (one, one, shape(2 * rows), shape(rows - tail), shape(tail), *state, *state),
         scalars=0,
         spec=HBM,
         scratch_shapes=[
@@ -204,11 +247,13 @@
 
     that_late, igrad, tgrad = after(that, igrad, tgrad)
     far_txt = inward(that_late)
+    relayed = relay_out(ihat_b)
     near_txt, igrad = call(
         raw_kernel, "near_text", (*tb, *img, near_txt, igrad), (one, one)
     )
-    ihat_late, near_txt, igrad = after(ihat, near_txt, igrad)
-    far_img = inward(ihat_late)
+    ihat_a, ihat_b, near_txt, igrad = after(ihat_a, ihat_b, near_txt, igrad)
+    far_img_a = inward(ihat_a)
+    far_img_b = inward(ihat_b, direct)
     cross_txt = swap(near_txt)
     igrad, tgrad = call(
         pair_kernel, "pair_tiles", (*tb, *img, *txt, pair, igrad, tgrad), (one, one)
@@ -217,17 +262,22 @@
         cross_kernel, "cross_text", (*tb, *img, cross_txt, igrad, ihat), (one, column)
     )
 
+    relayed, igrad = after(relayed, igrad)
+    relayed = relay_in(relayed)
     near_img, igrad = after(near_img, igrad)
     cross_img = swap(near_img)
     tgrad = call(tile_kernel, "near_image", (*tb, *txt, near_img, tgrad), one)
 
     far_txt, igrad, tgrad = after(far_txt, igrad, tgrad)
-    grad_image = last("last_text", *img, far_txt, igrad, ihat, inner_img, iinv)
+    grad_image = last("last_text", 1, *img, far_txt, igrad, ihat, inner_img, iinv)
     cross_img, grad_image = after(cross_img, grad_image)
+    tgrad = call(tile_kernel, "cross_image", (*tb, *txt, cross_img, tgrad), one)
     tgrad, inner_txt = call(
-        cross_kernel, "cross_image", (*tb, *txt, cross_img, tgrad, that), (one, column)
-    )
-    grad_text = last("last_image", *txt, far_img, tgrad, that, inner_txt, tinv)
+        cross_kernel, "far_image", (*tb, *txt, far_img_a, tgrad, that), (one, column)
+    )
+    grad_text = last(
+        "last_image", 2, *txt, far_img_b, relayed, tgrad, that, inner_txt, tinv
+    )
     return grad_image, grad_text
 
 

time: 73.1 us -> 74.9 us (1.025)
  starting transfers between devices: 37.2 us -> 44.6 us
  waiting for transfers between devices: 7.11 us -> 0.03 us
  Pallas kernels: 26.2 us -> 27.2 us
    ppermute x2 -> x5, starting transfers between devices: 11.8 us -> 19.4 us  [the longest x3 15.4 us: inward(): lax.ppermute(block, 'dp', [pair for pair in pairs if pair not in skip])]
    ppermute x2 -> x5, waiting for transfers between devices: 7.1 us -> 0.01 us  [the longest x3 0.01 us: inward(): lax.ppermute(block, 'dp', [pair for pair in pairs if pair not in skip])]
    pallas_call x9 -> x10, Pallas kernels: 26.2 us -> 27.2 us  [call(): pl.pallas_call(kernel, name=name, out_shape=outs, in_specs=[SMEM] * scala...]
  transfers between devices with their start and end apart: 7 -> 10, of which waited for: 1 -> 0; matrix products, arithmetic and copies ran while one was open for 0% -> 0% of each run, Pallas kernels for 32% -> 34%
where the time goes in v3:
time: 74.9 us; the launch traced here: 74.1 us
  starting transfers between devices  44.6 us (60%)
  Pallas kernels  27.2 us (36%)
  between operations  2.27 us (3%)
    pallas_call x10, Pallas kernels, call(): pl.pallas_call(kernel, name=name, out_shape=outs, in_specs=[SMEM] * scala...  27.2 us
    ppermute x3, starting transfers between devices, swap(): return lax.ppermute(block, 'dp', [(d, d ^ 1) for d in range(size)])  19.4 us
    ppermute x3, starting transfers between devices, inward(): lax.ppermute(block, 'dp', [pair for pair in pairs if pair not in skip])  15.4 us
    ppermute x2, starting transfers between devices, outward(): lax.ppermute(block, 'dp', [(d, (d + (2 if d % 2 else -2)) % size) for d i...  5.87 us
    ppermute x1, starting transfers between devices, relay_out(): lax.ppermute(block, 'dp', [(pair[0], mid) for pair, mid in zip(direct, vi...  3.11 us
  transfers between devices with their start and end apart: 10, of which 0 were waited for; matrix products, arithmetic and copies ran while one was open for 0% of the time, Pallas kernels for 34%

profile of v3, /device:TPU:1, one launch (start us, length us, event | category | flops | bytes accessed | tf_op | source)
XLA Modules:
  0.0 74.1 jit_solution(17554374655539463160)
XLA Ops:
  0.6 3.9 %collective-permute-start.2 = (f32[256,1152]{1,0:T(8,128)}, f32[256,1152]{1,0:T(8,128)S(1)}, u32[]{:S(2)}, u32[]{:S(2)}) collective-permute-start(f32[256,1152]{1,0:T(8,128)} %txt_in.1), channel_id=1, source_target_pairs={{0,510},{1,3},{2,0},{3,5},{4,2},{5,7},{6,4},{7,9},{8,6},{9,11},{10... | collective-permute-start | bytes 3538952 | tf_op jit(solution)/shard_map/ppermute | solution.py:184
  4.6 2.3 %unit_rows.1 = (f32[256,1152]{1,0:T(8,128)S(1)}, f32[256,1152]{1,0:T(8,128)S(1)}, f32[512,1152]{1,0:T(8,128)S(1)}, f32[128,1152]{1,0:T(8,128)S(1)}, f32[128,1152...) custom-call(f32[256,1152]{1,0:T(8,128)} %img_in.1, ...), custom_call_target="tpu_custom_call" | custom-call | flops 20000000000 | tf_op jit(solution)/shard_map/unit_rows/pallas_call | solution.py:156
  6.9 15.5 %collective-permute-start.4 = (f32[512,1152]{1,0:T(8,128)S(1)}, f32[512,1152]{1,0:T(8,128)S(1)}, u32[]{:S(2)}, u32[]{:S(2)}) collective-permute-start(f32[512,1152]{1,0:T(8,128)S(1)} %get-tuple-element.53), channel_id=1, source_target_pairs={{0,1},{1,0},{2,3},{3,2},{4,5},{5,4},{6,7},{7,6},{8,9},{9,8},{10,11... | collective-permute-start | bytes 7077896 | tf_op jit(solution)/shard_map/ppermute | solution.py:207
  22.4 3.1 %collective-permute-start.1 = (f32[128,1152]{1,0:T(8,128)S(1)}, f32[128,1152]{1,0:T(8,128)S(1)}, u32[]{:S(2)}, u32[]{:S(2)}) collective-permute-start(f32[128,1152]{1,0:T(8,128)S(1)} %get-tuple-element.68), channel_id=1, source_target_pairs={{510,14},{1,497},{126,142},{129,113},{254,270},{257,241},{382,398}... | collective-permute-start | bytes 1769480 | tf_op jit(solution)/shard_map/ppermute | solution.py:201
  25.5 1.9 %collective-permute-start = (f32[256,1152]{1,0:T(8,128)S(1)}, f32[256,1152]{1,0:T(8,128)S(1)}, u32[]{:S(2)}, u32[]{:S(2)}) collective-permute-start(f32[256,1152]{1,0:T(8,128)S(1)} %get-tuple-element.39.own.refs_2_), channel_id=1, source_target_pairs={{0,510},{1,3},{2,0},{3,5},{4,2},{5,7},{6,4},{7,9},{8,6},{9,11},{10... | collective-permute-start | bytes 3538952 | tf_op jit(solution)/shard_map/ppermute | solution.py:184
  28.8 4.4 %own_tiles.1 = (f32[256,1152]{1,0:T(8,128)S(1)}, f32[256,1152]{1,0:T(8,128)S(1)}) custom-call(f32[1]{0:T(128)S(6)} %copy.6.scale, f32[1]{0:T(128)S(6)} %copy.7.bias, bf16[256,1152]{1,0:T(8,128)(2,1)S(1)} %get-tuple-element.41.ihi.hi, bf16[256,1152]{1,0:T(8,128)(2,1)S(1)} %get-tuple-element.42.ilo.lo, bf16[256,1152]{1,0:T(8,128)(2,1)S(1)} %get-tuple-element.45.thi.hi, ...), custom_call_target="tpu_custom_call" | custom-call | flops 20000000000 | tf_op jit(solution)/shard_map/own_tiles/pallas_call | solution.py:156
  33.1 8.8 %collective-permute-start.6 = (f32[256,1152]{1,0:T(8,128)S(1)}, f32[256,1152]{1,0:T(8,128)S(1)}, u32[]{:S(2)}, u32[]{:S(2)}) collective-permute-start(f32[256,1152]{1,0:T(8,128)S(1)} %get-tuple-element.60.own.refs_3_), channel_id=1, source_target_pairs={{0,2},{1,511},{2,4},{3,1},{4,6},{5,3},{6,8},{7,5},{8,10},{9,7},{10... | collective-permute-start | bytes 3538952 | tf_op jit(solution)/shard_map/ppermute | solution.py:190
  41.9 0.0 collective-permute-done.2.raw
  42.0 2.4 %near_text.1 = (f32[256,1152]{1,0:T(8,128)S(1)}, f32[256,1152]{1,0:T(8,128)S(1)}) custom-call(f32[1]{0:T(128)S(6)} %copy.6.scale, f32[1]{0:T(128)S(6)} %copy.7.bias, bf16[256,1152]{1,0:T(8,128)(2,1)S(1)} %get-tuple-element.41.ihi.hi, bf16[256,1152]{1,0:T(8,128)(2,1)S(1)} %get-tuple-element.42.ilo.lo, f32[256,1152]{1,0:T(8,128)S(1)} %collective-permute-done.2.raw, ...), custom_call_target="tpu_custom_call" | custom-call | flops 20000000000 | tf_op jit(solution)/shard_map/near_text/pallas_call | solution.py:156
  44.4 1.9 %collective-permute-start.3 = (f32[256,1152]{1,0:T(8,128)S(1)}, f32[256,1152]{1,0:T(8,128)S(1)}, u32[]{:S(2)}, u32[]{:S(2)}) collective-permute-start(f32[256,1152]{1,0:T(8,128)S(1)} %get-tuple-element.52), channel_id=1, source_target_pairs={{0,1},{1,0},{2,3},{3,2},{4,5},{5,4},{6,7},{7,6},{8,9},{9,8},{10,11... | collective-permute-start | bytes 3538952 | tf_op jit(solution)/shard_map/ppermute | solution.py:207
  46.3 0.0 collective-permute-done.4.both
  46.3 5.3 %collective-permute-start.9 = (f32[128,1152]{1,0:T(8,128)S(1)}, f32[128,1152]{1,0:T(8,128)S(1)}, u32[]{:S(2)}, u32[]{:S(2)}) collective-permute-start(f32[128,1152]{1,0:T(8,128)S(1)} %get-tuple-element.70), channel_id=1, source_target_pairs={{0,2},{1,511},{2,4},{3,1},{4,6},{5,3},{6,8},{7,5},{8,10},{9,7},{10... | collective-permute-start | bytes 1769480 | tf_op jit(solution)/shard_map/ppermute | solution.py:190
  51.6 4.4 %pair_tiles.1 = (f32[256,1152]{1,0:T(8,128)S(1)}, f32[256,1152]{1,0:T(8,128)S(1)}) custom-call(f32[1]{0:T(128)S(6)} %copy.6.scale, f32[1]{0:T(128)S(6)} %copy.7.bias, bf16[256,1152]{1,0:T(8,128)(2,1)S(1)} %get-tuple-element.41.ihi.hi, bf16[256,1152]{1,0:T(8,128)(2,1)S(1)} %get-tuple-element.42.ilo.lo, bf16[256,1152]{1,0:T(8,128)(2,1)S(1)} %get-tuple-element.45.thi.hi, ...), custom_call_target="tpu_custom_call" | custom-call | flops 20000000000 | tf_op jit(solution)/shard_map/pair_tiles/pallas_call | solution.py:156
  56.0 0.0 collective-permute-done.3.hat
  56.0 1.3 %collective-permute-start.7 = (f32[128,1152]{1,0:T(8,128)S(1)}, f32[128,1152]{1,0:T(8,128)S(1)}, u32[]{:S(2)}, u32[]{:S(2)}) collective-permute-start(f32[128,1152]{1,0:T(8,128)S(1)} %get-tuple-element.68), channel_id=1, source_target_pairs={{0,2},{2,4},{3,1},{4,6},{5,3},{6,8},{7,5},{8,10},{9,7},{10,12},{11... | collective-permute-start | bytes 1769480 | tf_op jit(solution)/shard_map/ppermute | solution.py:190
  57.3 2.4 %cross_text.1 = (f32[256,1152]{1,0:T(8,128)S(1)}, f32[256,1]{1,0:T(8,128)S(1)}) custom-call(f32[1]{0:T(128)S(6)} %copy.6.scale, f32[1]{0:T(128)S(6)} %copy.7.bias, bf16[256,1152]{1,0:T(8,128)(2,1)S(1)} %get-tuple-element.41.ihi.hi, bf16[256,1152]{1,0:T(8,128)(2,1)S(1)} %get-tuple-element.42.ilo.lo, f32[256,1152]{1,0:T(8,128)S(1)} %collective-permute-done.3.hat, ...), custom_call_target="tpu_custom_call" | custom-call | flops 20000000000 | tf_op jit(solution)/shard_map/cross_text/pallas_call | solution.py:156
  59.7 0.0 collective-permute-done.1
  59.7 0.0 collective-permute-done.hat
  59.7 1.9 %collective-permute-start.5 = (f32[256,1152]{1,0:T(8,128)S(1)}, f32[256,1152]{1,0:T(8,128)S(1)}, u32[]{:S(2)}, u32[]{:S(2)}) collective-permute-start(f32[256,1152]{1,0:T(8,128)S(1)} %collective-permute-done.hat), channel_id=1, source_target_pairs={{0,1},{1,0},{2,3},{3,2},{4,5},{5,4},{6,7},{7,6},{8,9},{9,8},{10,11... | collective-permute-start | bytes 3538952 | tf_op jit(solution)/shard_map/ppermute | solution.py:207
  61.6 0.9 %collective-permute-start.8 = (f32[128,1152]{1,0:T(8,128)S(1)}, f32[128,1152]{1,0:T(8,128)S(1)}, u32[]{:S(2)}, u32[]{:S(2)}) collective-permute-start(f32[128,1152]{1,0:T(8,128)S(1)} %collective-permute-done.1), channel_id=1, source_target_pairs={{14,0},{497,511},{142,128},{113,127},{270,256},{241,255},{398,384}... | collective-permute-start | bytes 1769480 | tf_op jit(solution)/shard_map/ppermute | solution.py:204
  62.5 2.3 %near_image.1.grad = f32[256,1152]{1,0:T(8,128)S(1)} custom-call(f32[1]{0:T(128)S(6)} %copy.6.scale, f32[1]{0:T(128)S(6)} %copy.7.bias, bf16[256,1152]{1,0:T(8,128)(2,1)S(1)} %get-tuple-element.45.thi.hi, bf16[256,1152]{1,0:T(8,128)(2,1)S(1)} %get-tuple-element.46.tlo.lo, f32[256,1152]{1,0:T(8,128)S(1)} %collective-permute-done.hat, ...), custom_call_target="tpu_custom_call" | custom-call | flops 20000000000 | tf_op jit(solution)/shard_map/near_image/pallas_call | solution.py:156
  64.8 0.0 collective-permute-done.6.refs_0_
  64.8 3.0 %last_text.1 = f32[256,1152]{1,0:T(8,128)} custom-call(f32[1]{0:T(128)S(6)} %copy.6.scale, f32[1]{0:T(128)S(6)} %copy.7.bias, bf16[256,1152]{1,0:T(8,128)(2,1)S(1)} %get-tuple-element.41.ihi.hi, bf16[256,1152]{1,0:T(8,128)(2,1)S(1)} %get-tuple-element.42.ilo.lo, f32[256,1152]{1,0:T(8,128)S(1)} %collective-permute-done.6.refs_0_, ...), custom_call_target="tpu_custom_call" | custom-call | flops 1 | tf_op jit(solution)/shard_map/last_text/pallas_call | solution.py:156
  67.8 0.0 collective-permute-done.5.hat
  67.8 2.3 %cross_image.1.grad = f32[256,1152]{1,0:T(8,128)S(1)} custom-call(f32[1]{0:T(128)S(6)} %copy.6.scale, f32[1]{0:T(128)S(6)} %copy.7.bias, bf16[256,1152]{1,0:T(8,128)(2,1)S(1)} %get-tuple-element.45.thi.hi, bf16[256,1152]{1,0:T(8,128)(2,1)S(1)} %get-tuple-element.46.tlo.lo, f32[256,1152]{1,0:T(8,128)S(1)} %collective-permute-done.5.hat, ...), custom_call_target="tpu_custom_call" | custom-call | flops 1 | tf_op jit(solution)/shard_map/cross_image/pallas_call | solution.py:156
  70.1 0.0 collective-permute-done.9.hat
  70.1 1.9 %far_image.1 = (f32[256,1152]{1,0:T(8,128)S(1)}, f32[256,1]{1,0:T(8,128)S(1)}) custom-call(f32[1]{0:T(128)S(6)} %copy.6.scale, f32[1]{0:T(128)S(6)} %copy.7.bias, bf16[256,1152]{1,0:T(8,128)(2,1)S(1)} %get-tuple-element.45.thi.hi, bf16[256,1152]{1,0:T(8,128)(2,1)S(1)} %get-tuple-element.46.tlo.lo, f32[128,1152]{1,0:T(8,128)S(1)} %collective-permute-done.9.hat, ...), custom_call_target="tpu_custom_call" | custom-call | flops 1 | tf_op jit(solution)/shard_map/far_image/pallas_call | solution.py:156
  72.1 0.0 collective-permute-done.7.refs_0_
  72.1 0.0 collective-permute-done.8.refs_1_
  72.1 1.9 %last_image.1 = f32[256,1152]{1,0:T(8,128)} custom-call(f32[1]{0:T(128)S(6)} %copy.6.scale, f32[1]{0:T(128)S(6)} %copy.7.bias, bf16[256,1152]{1,0:T(8,128)(2,1)S(1)} %get-tuple-element.45.thi.hi, bf16[256,1152]{1,0:T(8,128)(2,1)S(1)} %get-tuple-element.46.tlo.lo, f32[128,1152]{1,0:T(8,128)S(1)} %collective-permute-done.7.refs_0_, ...), custom_call_target="tpu_custom_call" | custom-call | flops 20000000000 | tf_op jit(solution)/shard_map/last_image/pallas_call | solution.py:156
Async XLA Ops:
  0.6 41.3 %collective-permute-start.2 = (f32[256,1152]{1,0:T(8,128)}, f32[256,1152]{1,0:T(8,128)S(1)}, u32[]{:S(2)}, u32[]{:S(2)}) collective-permute-start(f32[256,1152]{1,0:T(8,128)} %txt_in.1), channel_id=1, source_target_pairs={{0,510},{1,3},{2,0},{3,5},{4,2},{5,7},{6,4},{7,9},{8,6},{9,11},{10... | collective-permute-start | bytes 3538952 | tf_op jit(solution)/shard_map/ppermute | solution.py:184
  6.9 39.4 %collective-permute-start.4 = (f32[512,1152]{1,0:T(8,128)S(1)}, f32[512,1152]{1,0:T(8,128)S(1)}, u32[]{:S(2)}, u32[]{:S(2)}) collective-permute-start(f32[512,1152]{1,0:T(8,128)S(1)} %get-tuple-element.53), channel_id=1, source_target_pairs={{0,1},{1,0},{2,3},{3,2},{4,5},{5,4},{6,7},{7,6},{8,9},{9,8},{10,11... | collective-permute-start | bytes 7077896 | tf_op jit(solution)/shard_map/ppermute | solution.py:207
  22.4 37.3 %collective-permute-start.1 = (f32[128,1152]{1,0:T(8,128)S(1)}, f32[128,1152]{1,0:T(8,128)S(1)}, u32[]{:S(2)}, u32[]{:S(2)}) collective-permute-start(f32[128,1152]{1,0:T(8,128)S(1)} %get-tuple-element.68), channel_id=1, source_target_pairs={{510,14},{1,497},{126,142},{129,113},{254,270},{257,241},{382,398}... | collective-permute-start | bytes 1769480 | tf_op jit(solution)/shard_map/ppermute | solution.py:201
  25.5 34.1 %collective-permute-start = (f32[256,1152]{1,0:T(8,128)S(1)}, f32[256,1152]{1,0:T(8,128)S(1)}, u32[]{:S(2)}, u32[]{:S(2)}) collective-permute-start(f32[256,1152]{1,0:T(8,128)S(1)} %get-tuple-element.39.own.refs_2_), channel_id=1, source_target_pairs={{0,510},{1,3},{2,0},{3,5},{4,2},{5,7},{6,4},{7,9},{8,6},{9,11},{10... | collective-permute-start | bytes 3538952 | tf_op jit(solution)/shard_map/ppermute | solution.py:184
  33.1 31.7 %collective-permute-start.6 = (f32[256,1152]{1,0:T(8,128)S(1)}, f32[256,1152]{1,0:T(8,128)S(1)}, u32[]{:S(2)}, u32[]{:S(2)}) collective-permute-start(f32[256,1152]{1,0:T(8,128)S(1)} %get-tuple-element.60.own.refs_3_), channel_id=1, source_target_pairs={{0,2},{1,511},{2,4},{3,1},{4,6},{5,3},{6,8},{7,5},{8,10},{9,7},{10... | collective-permute-start | bytes 3538952 | tf_op jit(solution)/shard_map/ppermute | solution.py:190
  44.4 11.6 %collective-permute-start.3 = (f32[256,1152]{1,0:T(8,128)S(1)}, f32[256,1152]{1,0:T(8,128)S(1)}, u32[]{:S(2)}, u32[]{:S(2)}) collective-permute-start(f32[256,1152]{1,0:T(8,128)S(1)} %get-tuple-element.52), channel_id=1, source_target_pairs={{0,1},{1,0},{2,3},{3,2},{4,5},{5,4},{6,7},{7,6},{8,9},{9,8},{10,11... | collective-permute-start | bytes 3538952 | tf_op jit(solution)/shard_map/ppermute | solution.py:207
  46.3 23.8 %collective-permute-start.9 = (f32[128,1152]{1,0:T(8,128)S(1)}, f32[128,1152]{1,0:T(8,128)S(1)}, u32[]{:S(2)}, u32[]{:S(2)}) collective-permute-start(f32[128,1152]{1,0:T(8,128)S(1)} %get-tuple-element.70), channel_id=1, source_target_pairs={{0,2},{1,511},{2,4},{3,1},{4,6},{5,3},{6,8},{7,5},{8,10},{9,7},{10... | collective-permute-start | bytes 1769480 | tf_op jit(solution)/shard_map/ppermute | solution.py:190
  56.0 16.1 %collective-permute-start.7 = (f32[128,1152]{1,0:T(8,128)S(1)}, f32[128,1152]{1,0:T(8,128)S(1)}, u32[]{:S(2)}, u32[]{:S(2)}) collective-permute-start(f32[128,1152]{1,0:T(8,128)S(1)} %get-tuple-element.68), channel_id=1, source_target_pairs={{0,2},{2,4},{3,1},{4,6},{5,3},{6,8},{7,5},{8,10},{9,7},{10,12},{11... | collective-permute-start | bytes 1769480 | tf_op jit(solution)/shard_map/ppermute | solution.py:190
  59.7 8.1 %collective-permute-start.5 = (f32[256,1152]{1,0:T(8,128)S(1)}, f32[256,1152]{1,0:T(8,128)S(1)}, u32[]{:S(2)}, u32[]{:S(2)}) collective-permute-start(f32[256,1152]{1,0:T(8,128)S(1)} %collective-permute-done.hat), channel_id=1, source_target_pairs={{0,1},{1,0},{2,3},{3,2},{4,5},{5,4},{6,7},{7,6},{8,9},{9,8},{10,11... | collective-permute-start | bytes 3538952 | tf_op jit(solution)/shard_map/ppermute | solution.py:207
  61.6 10.4 %collective-permute-start.8 = (f32[128,1152]{1,0:T(8,128)S(1)}, f32[128,1152]{1,0:T(8,128)S(1)}, u32[]{:S(2)}, u32[]{:S(2)}) collective-permute-start(f32[128,1152]{1,0:T(8,128)S(1)} %collective-permute-done.1), channel_id=1, source_target_pairs={{14,0},{497,511},{142,128},{113,127},{270,256},{241,255},{398,384}... | collective-permute-start | bytes 1769480 | tf_op jit(solution)/shard_map/ppermute | solution.py:204

commit v4 on v2

--- a/solution.py
+++ b/solution.py
@@ -49,7 +49,7 @@
     return product(split(coeff), y, NN)
 
 
-def unit_kernel(img_in, txt_in, ihat, that, both, *refs):
+def unit_kernel(img_in, txt_in, ihat, that, both, ihat_a, ihat_b, *refs):
     (iinv, ihi, ilo, tinv, thi, tlo, raw, sems) = refs
     rows = ihat.shape[0]
     part = rows // PARTS
@@ -71,6 +71,9 @@
         hat[...], inv[...] = unit(raw[n * rows : (n + 1) * rows])
         both[n * rows : (n + 1) * rows] = hat[...]
         hi[...], lo[...] = split(hat[...])
+        if n == 0:
+            ihat_a[...] = hat[: ihat_a.shape[0]]
+            ihat_b[...] = hat[ihat_a.shape[0] :]
 
 
 def own_kernel(scale, bias, ihi, ilo, thi, tlo, igrad, tgrad):
@@ -101,18 +104,36 @@
     inner[...] = jnp.sum(own[...] * total[...], axis=1, keepdims=True)
 
 
+def stacked(hi, lo, y_hi, y_lo, scale, bias):
+    rows = y_hi.shape[0]
+    mul = functools.partial(lax.dot_general, preferred_element_type=F32)
+    both = mul(hi, jnp.concatenate([y_hi, y_lo], axis=0), NT)
+    dots = both[:, :rows] + (both[:, rows:] + mul(lo, y_hi, NT))
+    coeff = jax.nn.sigmoid(scale * dots + bias)
+    top, rest = split(coeff)
+    left = jnp.concatenate([top, rest], axis=1)
+    right = jnp.concatenate([y_hi, y_hi], axis=0)
+    return dots, coeff, lambda here: (
+        mul(left, right[:, here], NN) + mul(top, y_lo[:, here], NN)
+    )
+
+
 def last_kernel(scale, bias, hi, lo, hat, grad, own, inner, inv, out, part, sems):
     y = split(hat[...])
-    dots = product((hi[...], lo[...]), y, NT)
-    coeff = jax.nn.sigmoid(scale[0] * dots + bias[0])
+    if 2 * hat.shape[0] <= hi.shape[0]:
+        dots, coeff, columns = stacked(hi[...], lo[...], *y, scale[0], bias[0])
+    else:
+        dots = product((hi[...], lo[...]), y, NT)
+        coeff = jax.nn.sigmoid(scale[0] * dots + bias[0])
+        halves = split(coeff)
+        columns = lambda here: product(halves, [half[:, here] for half in y], NN)
     along = inner[...] + jnp.sum(coeff * dots, axis=1, keepdims=True)
     factor = scale[0] * inv[...]
-    coeff = split(coeff)
     copies = []
     width = hat.shape[1]
     for at in range(0, width, COLUMNS):
         here = slice(at, min(at + COLUMNS, width))
-        total = grad[:, here] + product(coeff, [half[:, here] for half in y], NN)
+        total = grad[:, here] + columns(here)
         part[:, here] = (total - own[:, here] * along) * factor
         wide = pl.ds(at, here.stop - at)
         copies.append(
@@ -146,6 +167,7 @@
         return jax.ShapeDtypeStruct((height, wide), kind)
 
     one = shape(rows)
+    tail = rows // 2
     column = shape(rows, 1)
     state = (column, shape(rows, kind=BF16), shape(rows, kind=BF16))
     tb = (logit_scale, logit_bias)
@@ -184,11 +206,11 @@
         pltpu.with_memory_space_constraint(raw, pltpu.HBM)
         for raw in (image_embed, text_embed)
     ]
-    ihat, that, both, *rest = call(
+    ihat, that, both, ihat_a, ihat_b, *rest = call(
         unit_kernel,
         "unit_rows",
         in_hbm,
-        (one, one, shape(2 * rows), *state, *state),
+        (one, one, shape(2 * rows), shape(rows - tail), shape(tail), *state, *state),
         scalars=0,
         spec=HBM,
         scratch_shapes=[
@@ -207,8 +229,9 @@
     near_txt, igrad = call(
         raw_kernel, "near_text", (*tb, *img, near_txt, igrad), (one, one)
     )
-    ihat_late, near_txt, igrad = after(ihat, near_txt, igrad)
-    far_img = inward(ihat_late)
+    ihat_a, ihat_b, near_txt, igrad = after(ihat_a, ihat_b, near_txt, igrad)
+    far_img_a = inward(ihat_a)
+    far_img_b = inward(ihat_b)
     cross_txt = swap(near_txt)
     igrad, tgrad = call(
         pair_kernel, "pair_tiles", (*tb, *img, *txt, pair, igrad, tgrad), (one, one)
@@ -224,10 +247,11 @@
     far_txt, igrad, tgrad = after(far_txt, igrad, tgrad)
     grad_image = last("last_text", *img, far_txt, igrad, ihat, inner_img, iinv)
     cross_img, grad_image = after(cross_img, grad_image)
+    tgrad = call(tile_kernel, "cross_image", (*tb, *txt, cross_img, tgrad), one)
     tgrad, inner_txt = call(
-        cross_kernel, "cross_image", (*tb, *txt, cross_img, tgrad, that), (one, column)
-    )
-    grad_text = last("last_image", *txt, far_img, tgrad, that, inner_txt, tinv)
+        cross_kernel, "far_image", (*tb, *txt, far_img_a, tgrad, that), (one, column)
+    )
+    grad_text = last("last_image", *txt, far_img_b, tgrad, that, inner_txt, tinv)
     return grad_image, grad_text
 
 

time: 73.1 us -> 72 us (0.985)
  waiting for transfers between devices: 7.11 us -> 3.08 us
  starting transfers between devices: 37.2 us -> 39.1 us
  Pallas kernels: 26.2 us -> 27.2 us
    ppermute x2 -> x3, waiting for transfers between devices: 7.1 us -> 3.07 us  [inward(): lax.ppermute(block, 'dp', [(d, (d + (-2 if d % 2 else 2)) % size) for d i...]
    ppermute x2 -> x3, starting transfers between devices: 11.8 us -> 13.7 us  [inward(): lax.ppermute(block, 'dp', [(d, (d + (-2 if d % 2 else 2)) % size) for d i...]
    pallas_call x9 -> x10, Pallas kernels: 26.2 us -> 27.2 us  [call(): pl.pallas_call(kernel, name=name, out_shape=outs, in_specs=[SMEM] * scala...]
  transfers between devices with their start and end apart: 7 -> 8, of which waited for: 1 -> 1; matrix products, arithmetic and copies ran while one was open for 0% -> 0% of each run, Pallas kernels for 32% -> 35%
where the time goes in v4:
time: 72 us; the launch traced here: 71.7 us
  starting transfers between devices  39.1 us (54%)
  Pallas kernels  27.2 us (38%)
  waiting for transfers between devices  3.08 us (4%)
  between operations  2.24 us (3%)
    pallas_call x10, Pallas kernels, call(): pl.pallas_call(kernel, name=name, out_shape=outs, in_specs=[SMEM] * scala...  27.2 us
    ppermute x3, starting transfers between devices, swap(): return lax.ppermute(block, 'dp', [(d, d ^ 1) for d in range(size)])  19.5 us
    ppermute x3, starting transfers between devices, inward(): lax.ppermute(block, 'dp', [(d, (d + (-2 if d % 2 else 2)) % size) for d i...  13.7 us
    ppermute x2, starting transfers between devices, outward(): lax.ppermute(block, 'dp', [(d, (d + (2 if d % 2 else -2)) % size) for d i...  5.87 us
    ppermute x3, waiting for transfers between devices, inward(): lax.ppermute(block, 'dp', [(d, (d + (-2 if d % 2 else 2)) % size) for d i...  3.07 us
  transfers between devices with their start and end apart: 8, of which 1 were waited for; matrix products, arithmetic and copies ran while one was open for 0% of the time, Pallas kernels for 35%

profile of v4, /device:TPU:1, one launch (start us, length us, event | category | flops | bytes accessed | tf_op | source)
XLA Modules:
  0.0 71.7 jit_solution(3791071385304168609)
XLA Ops:
  0.6 3.9 %collective-permute-start.1 = (f32[256,1152]{1,0:T(8,128)}, f32[256,1152]{1,0:T(8,128)S(1)}, u32[]{:S(2)}, u32[]{:S(2)}) collective-permute-start(f32[256,1152]{1,0:T(8,128)} %txt_in.1), channel_id=1, source_target_pairs={{0,510},{1,3},{2,0},{3,5},{4,2},{5,7},{6,4},{7,9},{8,6},{9,11},{10... | collective-permute-start | bytes 3538952 | tf_op jit(solution)/shard_map/ppermute | solution.py:176
  4.6 2.3 %unit_rows.1 = (f32[256,1152]{1,0:T(8,128)S(1)}, f32[256,1152]{1,0:T(8,128)S(1)}, f32[512,1152]{1,0:T(8,128)S(1)}, f32[128,1152]{1,0:T(8,128)S(1)}, f32[128,1152...) custom-call(f32[256,1152]{1,0:T(8,128)} %img_in.1, ...), custom_call_target="tpu_custom_call" | custom-call | flops 20000000000 | tf_op jit(solution)/shard_map/unit_rows/pallas_call | solution.py:150
  6.9 15.5 %collective-permute-start.3 = (f32[512,1152]{1,0:T(8,128)S(1)}, f32[512,1152]{1,0:T(8,128)S(1)}, u32[]{:S(2)}, u32[]{:S(2)}) collective-permute-start(f32[512,1152]{1,0:T(8,128)S(1)} %get-tuple-element.51), channel_id=1, source_target_pairs={{0,1},{1,0},{2,3},{3,2},{4,5},{5,4},{6,7},{7,6},{8,9},{9,8},{10,11... | collective-permute-start | bytes 7077896 | tf_op jit(solution)/shard_map/ppermute | solution.py:186
  22.4 1.9 %collective-permute-start = (f32[256,1152]{1,0:T(8,128)S(1)}, f32[256,1152]{1,0:T(8,128)S(1)}, u32[]{:S(2)}, u32[]{:S(2)}) collective-permute-start(f32[256,1152]{1,0:T(8,128)S(1)} %get-tuple-element.37.own), channel_id=1, source_target_pairs={{0,510},{1,3},{2,0},{3,5},{4,2},{5,7},{6,4},{7,9},{8,6},{9,11},{10... | collective-permute-start | bytes 3538952 | tf_op jit(solution)/shard_map/ppermute | solution.py:176
  25.6 4.4 %own_tiles.1 = (f32[256,1152]{1,0:T(8,128)S(1)}, f32[256,1152]{1,0:T(8,128)S(1)}) custom-call(f32[1]{0:T(128)S(6)} %copy.6.scale, f32[1]{0:T(128)S(6)} %copy.7.bias, bf16[256,1152]{1,0:T(8,128)(2,1)S(1)} %get-tuple-element.38.ihi.hi, bf16[256,1152]{1,0:T(8,128)(2,1)S(1)} %get-tuple-element.39.ilo.lo, bf16[256,1152]{1,0:T(8,128)(2,1)S(1)} %get-tuple-element.43.thi.hi, ...), custom_call_target="tpu_custom_call" | custom-call | flops 20000000000 | tf_op jit(solution)/shard_map/own_tiles/pallas_call | solution.py:150
  30.0 8.8 %collective-permute-start.5 = (f32[256,1152]{1,0:T(8,128)S(1)}, f32[256,1152]{1,0:T(8,128)S(1)}, u32[]{:S(2)}, u32[]{:S(2)}) collective-permute-start(f32[256,1152]{1,0:T(8,128)S(1)} %get-tuple-element.57.own), channel_id=1, source_target_pairs={{0,2},{1,511},{2,4},{3,1},{4,6},{5,3},{6,8},{7,5},{8,10},{9,7},{10... | collective-permute-start | bytes 3538952 | tf_op jit(solution)/shard_map/ppermute | solution.py:181
  38.8 0.0 collective-permute-done.1.raw
  38.8 2.4 %near_text.1 = (f32[256,1152]{1,0:T(8,128)S(1)}, f32[256,1152]{1,0:T(8,128)S(1)}) custom-call(f32[1]{0:T(128)S(6)} %copy.6.scale, f32[1]{0:T(128)S(6)} %copy.7.bias, bf16[256,1152]{1,0:T(8,128)(2,1)S(1)} %get-tuple-element.38.ihi.hi, bf16[256,1152]{1,0:T(8,128)(2,1)S(1)} %get-tuple-element.39.ilo.lo, f32[256,1152]{1,0:T(8,128)S(1)} %collective-permute-done.1.raw, ...), custom_call_target="tpu_custom_call" | custom-call | flops 20000000000 | tf_op jit(solution)/shard_map/near_text/pallas_call | solution.py:150
  41.3 1.9 %collective-permute-start.2 = (f32[256,1152]{1,0:T(8,128)S(1)}, f32[256,1152]{1,0:T(8,128)S(1)}, u32[]{:S(2)}, u32[]{:S(2)}) collective-permute-start(f32[256,1152]{1,0:T(8,128)S(1)} %get-tuple-element.50), channel_id=1, source_target_pairs={{0,1},{1,0},{2,3},{3,2},{4,5},{5,4},{6,7},{7,6},{8,9},{9,8},{10,11... | collective-permute-start | bytes 3538952 | tf_op jit(solution)/shard_map/ppermute | solution.py:186
  43.2 3.0 %collective-permute-start.7 = (f32[128,1152]{1,0:T(8,128)S(1)}, f32[128,1152]{1,0:T(8,128)S(1)}, u32[]{:S(2)}, u32[]{:S(2)}) collective-permute-start(f32[128,1152]{1,0:T(8,128)S(1)} %get-tuple-element.66), channel_id=1, source_target_pairs={{0,2},{1,511},{2,4},{3,1},{4,6},{5,3},{6,8},{7,5},{8,10},{9,7},{10... | collective-permute-start | bytes 1769480 | tf_op jit(solution)/shard_map/ppermute | solution.py:181
  46.2 0.0 collective-permute-done.3.both
  46.2 1.9 %collective-permute-start.6 = (f32[128,1152]{1,0:T(8,128)S(1)}, f32[128,1152]{1,0:T(8,128)S(1)}, u32[]{:S(2)}, u32[]{:S(2)}) collective-permute-start(f32[128,1152]{1,0:T(8,128)S(1)} %get-tuple-element.65), channel_id=1, source_target_pairs={{0,2},{1,511},{2,4},{3,1},{4,6},{5,3},{6,8},{7,5},{8,10},{9,7},{10... | collective-permute-start | bytes 1769480 | tf_op jit(solution)/shard_map/ppermute | solution.py:181
  48.1 4.4 %pair_tiles.1 = (f32[256,1152]{1,0:T(8,128)S(1)}, f32[256,1152]{1,0:T(8,128)S(1)}) custom-call(f32[1]{0:T(128)S(6)} %copy.6.scale, f32[1]{0:T(128)S(6)} %copy.7.bias, bf16[256,1152]{1,0:T(8,128)(2,1)S(1)} %get-tuple-element.38.ihi.hi, bf16[256,1152]{1,0:T(8,128)(2,1)S(1)} %get-tuple-element.39.ilo.lo, bf16[256,1152]{1,0:T(8,128)(2,1)S(1)} %get-tuple-element.43.thi.hi, ...), custom_call_target="tpu_custom_call" | custom-call | flops 20000000000 | tf_op jit(solution)/shard_map/pair_tiles/pallas_call | solution.py:150
  52.5 0.0 collective-permute-done.2.hat
  52.5 2.4 %cross_text.1 = (f32[256,1152]{1,0:T(8,128)S(1)}, f32[256,1]{1,0:T(8,128)S(1)}) custom-call(f32[1]{0:T(128)S(6)} %copy.6.scale, f32[1]{0:T(128)S(6)} %copy.7.bias, bf16[256,1152]{1,0:T(8,128)(2,1)S(1)} %get-tuple-element.38.ihi.hi, bf16[256,1152]{1,0:T(8,128)(2,1)S(1)} %get-tuple-element.39.ilo.lo, f32[256,1152]{1,0:T(8,128)S(1)} %collective-permute-done.2.hat, ...), custom_call_target="tpu_custom_call" | custom-call | flops 20000000000 | tf_op jit(solution)/shard_map/cross_text/pallas_call | solution.py:150
  54.9 0.0 collective-permute-done.hat
  54.9 2.1 %collective-permute-start.4 = (f32[256,1152]{1,0:T(8,128)S(1)}, f32[256,1152]{1,0:T(8,128)S(1)}, u32[]{:S(2)}, u32[]{:S(2)}) collective-permute-start(f32[256,1152]{1,0:T(8,128)S(1)} %collective-permute-done.hat), channel_id=1, source_target_pairs={{0,1},{1,0},{2,3},{3,2},{4,5},{5,4},{6,7},{7,6},{8,9},{9,8},{10,11... | collective-permute-start | bytes 3538952 | tf_op jit(solution)/shard_map/ppermute | solution.py:186
  57.0 2.3 %near_image.1.grad = f32[256,1152]{1,0:T(8,128)S(1)} custom-call(f32[1]{0:T(128)S(6)} %copy.6.scale, f32[1]{0:T(128)S(6)} %copy.7.bias, bf16[256,1152]{1,0:T(8,128)(2,1)S(1)} %get-tuple-element.43.thi.hi, bf16[256,1152]{1,0:T(8,128)(2,1)S(1)} %get-tuple-element.44.tlo.lo, f32[256,1152]{1,0:T(8,128)S(1)} %collective-permute-done.hat, ...), custom_call_target="tpu_custom_call" | custom-call | flops 20000000000 | tf_op jit(solution)/shard_map/near_image/pallas_call | solution.py:150
  59.3 0.0 collective-permute-done.5.hat
  59.3 3.0 %last_text.1 = f32[256,1152]{1,0:T(8,128)} custom-call(f32[1]{0:T(128)S(6)} %copy.6.scale, f32[1]{0:T(128)S(6)} %copy.7.bias, bf16[256,1152]{1,0:T(8,128)(2,1)S(1)} %get-tuple-element.38.ihi.hi, bf16[256,1152]{1,0:T(8,128)(2,1)S(1)} %get-tuple-element.39.ilo.lo, f32[256,1152]{1,0:T(8,128)S(1)} %collective-permute-done.5.hat, ...), custom_call_target="tpu_custom_call" | custom-call | flops 20000000000 | tf_op jit(solution)/shard_map/last_text/pallas_call | solution.py:150
  62.3 0.0 collective-permute-done.4.hat
  62.3 2.3 %cross_image.1.grad = f32[256,1152]{1,0:T(8,128)S(1)} custom-call(f32[1]{0:T(128)S(6)} %copy.6.scale, f32[1]{0:T(128)S(6)} %copy.7.bias, bf16[256,1152]{1,0:T(8,128)(2,1)S(1)} %get-tuple-element.43.thi.hi, bf16[256,1152]{1,0:T(8,128)(2,1)S(1)} %get-tuple-element.44.tlo.lo, f32[256,1152]{1,0:T(8,128)S(1)} %collective-permute-done.4.hat, ...), custom_call_target="tpu_custom_call" | custom-call | flops 20000000000 | tf_op jit(solution)/shard_map/cross_image/pallas_call | solution.py:150
  64.6 0.0 collective-permute-done.7.hat
  64.6 1.9 %far_image.1 = (f32[256,1152]{1,0:T(8,128)S(1)}, f32[256,1]{1,0:T(8,128)S(1)}) custom-call(f32[1]{0:T(128)S(6)} %copy.6.scale, f32[1]{0:T(128)S(6)} %copy.7.bias, bf16[256,1152]{1,0:T(8,128)(2,1)S(1)} %get-tuple-element.43.thi.hi, bf16[256,1152]{1,0:T(8,128)(2,1)S(1)} %get-tuple-element.44.tlo.lo, f32[128,1152]{1,0:T(8,128)S(1)} %collective-permute-done.7.hat, ...), custom_call_target="tpu_custom_call" | custom-call | flops 20000000000 | tf_op jit(solution)/shard_map/far_image/pallas_call | solution.py:150
  66.6 3.1 %collective-permute-done.6.hat = f32[128,1152]{1,0:T(8,128)S(1)} collective-permute-done((f32[128,1152]{1,0:T(8,128)S(1)}, f32[128,1152]{1,0:T(8,128)S(1)}, u32[]{:S(2)}, u32[]{:S(2)}) %collective-permute-start.6) | collective-permute-done | bytes 589856 | tf_op jit(solution)/shard_map/ppermute | solution.py:181
  69.6 1.9 %last_image.1 = f32[256,1152]{1,0:T(8,128)} custom-call(f32[1]{0:T(128)S(6)} %copy.6.scale, f32[1]{0:T(128)S(6)} %copy.7.bias, bf16[256,1152]{1,0:T(8,128)(2,1)S(1)} %get-tuple-element.43.thi.hi, bf16[256,1152]{1,0:T(8,128)(2,1)S(1)} %get-tuple-element.44.tlo.lo, f32[128,1152]{1,0:T(8,128)S(1)} %collective-permute-done.6.hat, ...), custom_call_target="tpu_custom_call" | custom-call | flops 20000000000 | tf_op jit(solution)/shard_map/last_image/pallas_call | solution.py:150
Async XLA Ops:
  0.6 38.2 %collective-permute-start.1 = (f32[256,1152]{1,0:T(8,128)}, f32[256,1152]{1,0:T(8,128)S(1)}, u32[]{:S(2)}, u32[]{:S(2)}) collective-permute-start(f32[256,1152]{1,0:T(8,128)} %txt_in.1), channel_id=1, source_target_pairs={{0,510},{1,3},{2,0},{3,5},{4,2},{5,7},{6,4},{7,9},{8,6},{9,11},{10... | collective-permute-start | bytes 3538952 | tf_op jit(solution)/shard_map/ppermute | solution.py:176
  6.9 39.3 %collective-permute-start.3 = (f32[512,1152]{1,0:T(8,128)S(1)}, f32[512,1152]{1,0:T(8,128)S(1)}, u32[]{:S(2)}, u32[]{:S(2)}) collective-permute-start(f32[512,1152]{1,0:T(8,128)S(1)} %get-tuple-element.51), channel_id=1, source_target_pairs={{0,1},{1,0},{2,3},{3,2},{4,5},{5,4},{6,7},{7,6},{8,9},{9,8},{10,11... | collective-permute-start | bytes 7077896 | tf_op jit(solution)/shard_map/ppermute | solution.py:186
  22.4 32.5 %collective-permute-start = (f32[256,1152]{1,0:T(8,128)S(1)}, f32[256,1152]{1,0:T(8,128)S(1)}, u32[]{:S(2)}, u32[]{:S(2)}) collective-permute-start(f32[256,1152]{1,0:T(8,128)S(1)} %get-tuple-element.37.own), channel_id=1, source_target_pairs={{0,510},{1,3},{2,0},{3,5},{4,2},{5,7},{6,4},{7,9},{8,6},{9,11},{10... | collective-permute-start | bytes 3538952 | tf_op jit(solution)/shard_map/ppermute | solution.py:176
  30.0 29.3 %collective-permute-start.5 = (f32[256,1152]{1,0:T(8,128)S(1)}, f32[256,1152]{1,0:T(8,128)S(1)}, u32[]{:S(2)}, u32[]{:S(2)}) collective-permute-start(f32[256,1152]{1,0:T(8,128)S(1)} %get-tuple-element.57.own), channel_id=1, source_target_pairs={{0,2},{1,511},{2,4},{3,1},{4,6},{5,3},{6,8},{7,5},{8,10},{9,7},{10... | collective-permute-start | bytes 3538952 | tf_op jit(solution)/shard_map/ppermute | solution.py:181
  41.3 11.3 %collective-permute-start.2 = (f32[256,1152]{1,0:T(8,128)S(1)}, f32[256,1152]{1,0:T(8,128)S(1)}, u32[]{:S(2)}, u32[]{:S(2)}) collective-permute-start(f32[256,1152]{1,0:T(8,128)S(1)} %get-tuple-element.50), channel_id=1, source_target_pairs={{0,1},{1,0},{2,3},{3,2},{4,5},{5,4},{6,7},{7,6},{8,9},{9,8},{10,11... | collective-permute-start | bytes 3538952 | tf_op jit(solution)/shard_map/ppermute | solution.py:186
  43.2 21.4 %collective-permute-start.7 = (f32[128,1152]{1,0:T(8,128)S(1)}, f32[128,1152]{1,0:T(8,128)S(1)}, u32[]{:S(2)}, u32[]{:S(2)}) collective-permute-start(f32[128,1152]{1,0:T(8,128)S(1)} %get-tuple-element.66), channel_id=1, source_target_pairs={{0,2},{1,511},{2,4},{3,1},{4,6},{5,3},{6,8},{7,5},{8,10},{9,7},{10... | collective-permute-start | bytes 1769480 | tf_op jit(solution)/shard_map/ppermute | solution.py:181
  46.2 23.4 %collective-permute-start.6 = (f32[128,1152]{1,0:T(8,128)S(1)}, f32[128,1152]{1,0:T(8,128)S(1)}, u32[]{:S(2)}, u32[]{:S(2)}) collective-permute-start(f32[128,1152]{1,0:T(8,128)S(1)} %get-tuple-element.65), channel_id=1, source_target_pairs={{0,2},{1,511},{2,4},{3,1},{4,6},{5,3},{6,8},{7,5},{8,10},{9,7},{10... | collective-permute-start | bytes 1769480 | tf_op jit(solution)/shard_map/ppermute | solution.py:181
  54.9 7.4 %collective-permute-start.4 = (f32[256,1152]{1,0:T(8,128)S(1)}, f32[256,1152]{1,0:T(8,128)S(1)}, u32[]{:S(2)}, u32[]{:S(2)}) collective-permute-start(f32[256,1152]{1,0:T(8,128)S(1)} %collective-permute-done.hat), channel_id=1, source_target_pairs={{0,1},{1,0},{2,3},{3,2},{4,5},{5,4},{6,7},{7,6},{8,9},{9,8},{10,11... | collective-permute-start | bytes 3538952 | tf_op jit(solution)/shard_map/ppermute | solution.py:186

commit v5 on v3

--- a/solution.py
+++ b/solution.py
@@ -14,8 +14,7 @@
 HBM = pl.BlockSpec(memory_space=pltpu.HBM)
 PARTS = 4
 COLUMNS = 256
-SEAM = 128
-LATE = ("last_text", "cross_image", "far_image")
+HINTS = {"last_text": 1, "cross_image": 1, "far_image": 1}
 NT = (((1,), (1,)), ((), ()))
 NN = (((1,), (0,)), ((), ()))
 
@@ -95,8 +94,10 @@
     tile_kernel(scale, bias, hi, lo, hat, grad, total)
 
 
-def pair_kernel(scale, bias, ihi, ilo, thi, tlo, both, igrad, tgrad, itotal, ttotal):
+def pair_kernel(scale, bias, ihi, ilo, thi, tlo, both, igrad, tgrad, *outs):
+    itotal, ttotal, passed = outs
     rows = igrad.shape[0]
+    passed[...] = both[rows - passed.shape[0] : rows]
     tile_kernel(scale, bias, ihi, ilo, both.at[rows:], igrad, itotal)
     tile_kernel(scale, bias, thi, tlo, both.at[:rows], tgrad, ttotal)
 
@@ -161,7 +162,7 @@
         out_specs=jax.tree.map(lambda _: out_spec, outs),
         compiler_params=pltpu.CompilerParams(vmem_limit_bytes=24 * 2**20),
         cost_estimate=pl.CostEstimate(
-            flops=1 if name in LATE else 2 * 10**10, bytes_accessed=0, transcendentals=0
+            flops=HINTS.get(name, 2 * 10**10), bytes_accessed=0, transcendentals=0
         ),
         **extra,
     )(*operands)
@@ -188,20 +189,6 @@
     def inward(block, skip=()):
         pairs = [(d, (d + (-2 if d % 2 else 2)) % size) for d in range(size)]
         return lax.ppermute(block, "dp", [pair for pair in pairs if pair not in skip])
-
-    seams = range(0, size, SEAM)
-    direct = [
-        pair
-        for at in seams
-        for pair in (((at - 2) % size, at), (at + 1, (at - 1) % size))
-    ]
-    via = [mid for at in seams for mid in ((at + 14) % size, (at - 15) % size)]
-
-    def relay_out(block):
-        return lax.ppermute(block, "dp", [(pair[0], mid) for pair, mid in zip(direct, via)])
-
-    def relay_in(block):
-        return lax.ppermute(block, "dp", [(mid, pair[1]) for pair, mid in zip(direct, via)])
 
     def swap(block):
         return lax.ppermute(block, "dp", [(d, d ^ 1) for d in range(size)])
@@ -247,23 +234,24 @@
 
     that_late, igrad, tgrad = after(that, igrad, tgrad)
     far_txt = inward(that_late)
-    relayed = relay_out(ihat_b)
     near_txt, igrad = call(
         raw_kernel, "near_text", (*tb, *img, near_txt, igrad), (one, one)
     )
     ihat_a, ihat_b, near_txt, igrad = after(ihat_a, ihat_b, near_txt, igrad)
     far_img_a = inward(ihat_a)
-    far_img_b = inward(ihat_b, direct)
+    far_img_b = inward(ihat_b, [(1, size - 1)])
     cross_txt = swap(near_txt)
-    igrad, tgrad = call(
-        pair_kernel, "pair_tiles", (*tb, *img, *txt, pair, igrad, tgrad), (one, one)
-    )
+    igrad, tgrad, passed = call(
+        pair_kernel,
+        "pair_tiles",
+        (*tb, *img, *txt, pair, igrad, tgrad),
+        (one, one, shape(tail)),
+    )
+    far_img_c = lax.ppermute(passed, "dp", [(0, size - 1)])
     igrad, inner_img = call(
         cross_kernel, "cross_text", (*tb, *img, cross_txt, igrad, ihat), (one, column)
     )
 
-    relayed, igrad = after(relayed, igrad)
-    relayed = relay_in(relayed)
     near_img, igrad = after(near_img, igrad)
     cross_img = swap(near_img)
     tgrad = call(tile_kernel, "near_image", (*tb, *txt, near_img, tgrad), one)
@@ -276,7 +264,7 @@
         cross_kernel, "far_image", (*tb, *txt, far_img_a, tgrad, that), (one, column)
     )
     grad_text = last(
-        "last_image", 2, *txt, far_img_b, relayed, tgrad, that, inner_txt, tinv
+        "last_image", 2, *txt, far_img_b, far_img_c, tgrad, that, inner_txt, tinv
     )
     return grad_image, grad_text
 

time: 74.9 us -> 71.1 us (0.949)
  the two profiles are of different devices: /device:TPU:1 before, /device:TPU:0 now
where the time goes in v5:
time: 71.1 us; the launch traced here: 70.7 us
  starting transfers between devices  41.1 us (58%)
  Pallas kernels  27.3 us (38%)
  between operations  2.26 us (3%)
    pallas_call x10, Pallas kernels, call(): pl.pallas_call(kernel, name=name, out_shape=outs, in_specs=[SMEM] * scala...  27.3 us
    ppermute x2, starting transfers between devices, outward(): lax.ppermute(block, 'dp', [(d, (d + (2 if d % 2 else -2)) % size) for d i...  13.4 us
    ppermute x3, starting transfers between devices, swap(): return lax.ppermute(block, 'dp', [(d, d ^ 1) for d in range(size)])  11.6 us
    ppermute x1, starting transfers between devices, body(): far_img_c = lax.ppermute(passed, 'dp', [(0, size - 1)])  9.2 us
    ppermute x3, starting transfers between devices, inward(): lax.ppermute(block, 'dp', [pair for pair in pairs if pair not in skip])  6.95 us
  transfers between devices with their start and end apart: 9, of which 0 were waited for; matrix products, arithmetic and copies ran while one was open for 0% of the time, Pallas kernels for 36%

profile of v5, /device:TPU:0, one launch (start us, length us, event | category | flops | bytes accessed | tf_op | source)
XLA Modules:
  0.0 70.7 jit_solution(11884881392163916846)
XLA Ops:
  0.6 10.7 %collective-permute-start.1 = (f32[256,1152]{1,0:T(8,128)}, f32[256,1152]{1,0:T(8,128)S(1)}, u32[]{:S(2)}, u32[]{:S(2)}) collective-permute-start(f32[256,1152]{1,0:T(8,128)} %txt_in.1), channel_id=1, source_target_pairs={{0,510},{1,3},{2,0},{3,5},{4,2},{5,7},{6,4},{7,9},{8,6},{9,11},{10... | collective-permute-start | bytes 3538952 | tf_op jit(solution)/shard_map/ppermute | solution.py:185
  11.3 2.3 %unit_rows.1 = (f32[256,1152]{1,0:T(8,128)S(1)}, f32[256,1152]{1,0:T(8,128)S(1)}, f32[512,1152]{1,0:T(8,128)S(1)}, f32[128,1152]{1,0:T(8,128)S(1)}, f32[128,1152...) custom-call(f32[256,1152]{1,0:T(8,128)} %img_in.1, ...), custom_call_target="tpu_custom_call" | custom-call | flops 20000000000 | tf_op jit(solution)/shard_map/unit_rows/pallas_call | solution.py:157
  13.6 1.9 %collective-permute-start.3 = (f32[512,1152]{1,0:T(8,128)S(1)}, f32[512,1152]{1,0:T(8,128)S(1)}, u32[]{:S(2)}, u32[]{:S(2)}) collective-permute-start(f32[512,1152]{1,0:T(8,128)S(1)} %get-tuple-element.52), channel_id=1, source_target_pairs={{0,1},{1,0},{2,3},{3,2},{4,5},{5,4},{6,7},{7,6},{8,9},{9,8},{10,11... | collective-permute-start | bytes 7077896 | tf_op jit(solution)/shard_map/ppermute | solution.py:194
  15.6 2.7 %collective-permute-start = (f32[256,1152]{1,0:T(8,128)S(1)}, f32[256,1152]{1,0:T(8,128)S(1)}, u32[]{:S(2)}, u32[]{:S(2)}) collective-permute-start(f32[256,1152]{1,0:T(8,128)S(1)} %get-tuple-element.38.own.refs_2_), channel_id=1, source_target_pairs={{0,510},{1,3},{2,0},{3,5},{4,2},{5,7},{6,4},{7,9},{8,6},{9,11},{10... | collective-permute-start | bytes 3538952 | tf_op jit(solution)/shard_map/ppermute | solution.py:185
  19.6 4.4 %own_tiles.1 = (f32[256,1152]{1,0:T(8,128)S(1)}, f32[256,1152]{1,0:T(8,128)S(1)}) custom-call(f32[1]{0:T(128)S(6)} %copy.6.scale, f32[1]{0:T(128)S(6)} %copy.7.bias, bf16[256,1152]{1,0:T(8,128)(2,1)S(1)} %get-tuple-element.39.ihi.hi, bf16[256,1152]{1,0:T(8,128)(2,1)S(1)} %get-tuple-element.40.ilo.lo, bf16[256,1152]{1,0:T(8,128)(2,1)S(1)} %get-tuple-element.44.thi.hi, ...), custom_call_target="tpu_custom_call" | custom-call | flops 20000000000 | tf_op jit(solution)/shard_map/own_tiles/pallas_call | solution.py:157
  24.0 3.1 %collective-permute-start.5 = (f32[256,1152]{1,0:T(8,128)S(1)}, f32[256,1152]{1,0:T(8,128)S(1)}, u32[]{:S(2)}, u32[]{:S(2)}) collective-permute-start(f32[256,1152]{1,0:T(8,128)S(1)} %get-tuple-element.58.own.refs_3_), channel_id=1, source_target_pairs={{0,2},{1,511},{2,4},{3,1},{4,6},{5,3},{6,8},{7,5},{8,10},{9,7},{10... | collective-permute-start | bytes 3538952 | tf_op jit(solution)/shard_map/ppermute | solution.py:191
  27.1 0.0 collective-permute-done.1.raw
  27.1 2.4 %near_text.1 = (f32[256,1152]{1,0:T(8,128)S(1)}, f32[256,1152]{1,0:T(8,128)S(1)}) custom-call(f32[1]{0:T(128)S(6)} %copy.6.scale, f32[1]{0:T(128)S(6)} %copy.7.bias, bf16[256,1152]{1,0:T(8,128)(2,1)S(1)} %get-tuple-element.39.ihi.hi, bf16[256,1152]{1,0:T(8,128)(2,1)S(1)} %get-tuple-element.40.ilo.lo, f32[256,1152]{1,0:T(8,128)S(1)} %collective-permute-done.1.raw, ...), custom_call_target="tpu_custom_call" | custom-call | flops 20000000000 | tf_op jit(solution)/shard_map/near_text/pallas_call | solution.py:157
  29.5 7.3 %collective-permute-start.2 = (f32[256,1152]{1,0:T(8,128)S(1)}, f32[256,1152]{1,0:T(8,128)S(1)}, u32[]{:S(2)}, u32[]{:S(2)}) collective-permute-start(f32[256,1152]{1,0:T(8,128)S(1)} %get-tuple-element.51), channel_id=1, source_target_pairs={{0,1},{1,0},{2,3},{3,2},{4,5},{5,4},{6,7},{7,6},{8,9},{9,8},{10,11... | collective-permute-start | bytes 3538952 | tf_op jit(solution)/shard_map/ppermute | solution.py:194
  36.8 1.9 %collective-permute-start.8 = (f32[128,1152]{1,0:T(8,128)S(1)}, f32[128,1152]{1,0:T(8,128)S(1)}, u32[]{:S(2)}, u32[]{:S(2)}) collective-permute-start(f32[128,1152]{1,0:T(8,128)S(1)} %get-tuple-element.68), channel_id=1, source_target_pairs={{0,2},{1,511},{2,4},{3,1},{4,6},{5,3},{6,8},{7,5},{8,10},{9,7},{10... | collective-permute-start | bytes 1769480 | tf_op jit(solution)/shard_map/ppermute | solution.py:191
  38.7 0.0 collective-permute-done.3.both
  38.7 1.9 %collective-permute-start.6 = (f32[128,1152]{1,0:T(8,128)S(1)}, f32[128,1152]{1,0:T(8,128)S(1)}, u32[]{:S(2)}, u32[]{:S(2)}) collective-permute-start(f32[128,1152]{1,0:T(8,128)S(1)} %get-tuple-element.66), channel_id=1, source_target_pairs={{0,2},{2,4},{3,1},{4,6},{5,3},{6,8},{7,5},{8,10},{9,7},{10,12},{11... | collective-permute-start | bytes 1769480 | tf_op jit(solution)/shard_map/ppermute | solution.py:191
  40.7 4.4 %pair_tiles.1 = (f32[256,1152]{1,0:T(8,128)S(1)}, f32[256,1152]{1,0:T(8,128)S(1)}, f32[128,1152]{1,0:T(8,128)S(1)}) custom-call(f32[1]{0:T(128)S(6)} %copy.6.scale, f32[1]{0:T(128)S(6)} %copy.7.bias, bf16[256,1152]{1,0:T(8,128)(2,1)S(1)} %get-tuple-element.39.ihi.hi, bf16[256,1152]{1,0:T(8,128)(2,1)S(1)} %get-tuple-element.40.ilo.lo, ...), custom_call_target="tpu_custom_call" | custom-call | flops 20000000000 | tf_op jit(solution)/shard_map/pair_tiles/pallas_call | solution.py:157
  45.1 0.0 collective-permute-done.2.hat
  45.1 2.4 %cross_text.1 = (f32[256,1152]{1,0:T(8,128)S(1)}, f32[256,1]{1,0:T(8,128)S(1)}) custom-call(f32[1]{0:T(128)S(6)} %copy.6.scale, f32[1]{0:T(128)S(6)} %copy.7.bias, bf16[256,1152]{1,0:T(8,128)(2,1)S(1)} %get-tuple-element.39.ihi.hi, bf16[256,1152]{1,0:T(8,128)(2,1)S(1)} %get-tuple-element.40.ilo.lo, f32[256,1152]{1,0:T(8,128)S(1)} %collective-permute-done.2.hat, ...), custom_call_target="tpu_custom_call" | custom-call | flops 20000000000 | tf_op jit(solution)/shard_map/cross_text/pallas_call | solution.py:157
  47.5 0.0 collective-permute-done.hat
  47.5 2.4 %collective-permute-start.4 = (f32[256,1152]{1,0:T(8,128)S(1)}, f32[256,1152]{1,0:T(8,128)S(1)}, u32[]{:S(2)}, u32[]{:S(2)}) collective-permute-start(f32[256,1152]{1,0:T(8,128)S(1)} %collective-permute-done.hat), channel_id=1, source_target_pairs={{0,1},{1,0},{2,3},{3,2},{4,5},{5,4},{6,7},{7,6},{8,9},{9,8},{10,11... | collective-permute-start | bytes 3538952 | tf_op jit(solution)/shard_map/ppermute | solution.py:194
  49.9 9.2 %collective-permute-start.7 = (f32[128,1152]{1,0:T(8,128)S(1)}, f32[128,1152]{1,0:T(8,128)S(1)}, u32[]{:S(2)}, u32[]{:S(2)}) collective-permute-start(f32[128,1152]{1,0:T(8,128)S(1)} %get-tuple-element.67), channel_id=1, source_target_pairs={{0,511}} | collective-permute-start | bytes 1769480 | tf_op jit(solution)/shard_map/ppermute | solution.py:250
  59.1 2.3 %near_image.1.grad = f32[256,1152]{1,0:T(8,128)S(1)} custom-call(f32[1]{0:T(128)S(6)} %copy.6.scale, f32[1]{0:T(128)S(6)} %copy.7.bias, bf16[256,1152]{1,0:T(8,128)(2,1)S(1)} %get-tuple-element.44.thi.hi, bf16[256,1152]{1,0:T(8,128)(2,1)S(1)} %get-tuple-element.45.tlo.lo, f32[256,1152]{1,0:T(8,128)S(1)} %collective-permute-done.hat, ...), custom_call_target="tpu_custom_call" | custom-call | flops 20000000000 | tf_op jit(solution)/shard_map/near_image/pallas_call | solution.py:157
  61.4 0.0 collective-permute-done.5.refs_0_
  61.4 3.0 %last_text.1 = f32[256,1152]{1,0:T(8,128)} custom-call(f32[1]{0:T(128)S(6)} %copy.6.scale, f32[1]{0:T(128)S(6)} %copy.7.bias, bf16[256,1152]{1,0:T(8,128)(2,1)S(1)} %get-tuple-element.39.ihi.hi, bf16[256,1152]{1,0:T(8,128)(2,1)S(1)} %get-tuple-element.40.ilo.lo, f32[256,1152]{1,0:T(8,128)S(1)} %collective-permute-done.5.refs_0_, ...), custom_call_target="tpu_custom_call" | custom-call | flops 1 | tf_op jit(solution)/shard_map/last_text/pallas_call | solution.py:157
  64.4 0.0 collective-permute-done.4.hat
  64.4 2.3 %cross_image.1.grad = f32[256,1152]{1,0:T(8,128)S(1)} custom-call(f32[1]{0:T(128)S(6)} %copy.6.scale, f32[1]{0:T(128)S(6)} %copy.7.bias, bf16[256,1152]{1,0:T(8,128)(2,1)S(1)} %get-tuple-element.44.thi.hi, bf16[256,1152]{1,0:T(8,128)(2,1)S(1)} %get-tuple-element.45.tlo.lo, f32[256,1152]{1,0:T(8,128)S(1)} %collective-permute-done.4.hat, ...), custom_call_target="tpu_custom_call" | custom-call | flops 1 | tf_op jit(solution)/shard_map/cross_image/pallas_call | solution.py:157
  66.7 0.0 collective-permute-done.8.hat
  66.7 1.9 %far_image.1 = (f32[256,1152]{1,0:T(8,128)S(1)}, f32[256,1]{1,0:T(8,128)S(1)}) custom-call(f32[1]{0:T(128)S(6)} %copy.6.scale, f32[1]{0:T(128)S(6)} %copy.7.bias, bf16[256,1152]{1,0:T(8,128)(2,1)S(1)} %get-tuple-element.44.thi.hi, bf16[256,1152]{1,0:T(8,128)(2,1)S(1)} %get-tuple-element.45.tlo.lo, f32[128,1152]{1,0:T(8,128)S(1)} %collective-permute-done.8.hat, ...), custom_call_target="tpu_custom_call" | custom-call | flops 1 | tf_op jit(solution)/shard_map/far_image/pallas_call | solution.py:157
  68.6 0.0 collective-permute-done.6.refs_0_
  68.6 0.0 collective-permute-done.7.refs_1_
  68.6 1.9 %last_image.1 = f32[256,1152]{1,0:T(8,128)} custom-call(f32[1]{0:T(128)S(6)} %copy.6.scale, f32[1]{0:T(128)S(6)} %copy.7.bias, bf16[256,1152]{1,0:T(8,128)(2,1)S(1)} %get-tuple-element.44.thi.hi, bf16[256,1152]{1,0:T(8,128)(2,1)S(1)} %get-tuple-element.45.tlo.lo, f32[128,1152]{1,0:T(8,128)S(1)} %collective-permute-done.6.refs_0_, ...), custom_call_target="tpu_custom_call" | custom-call | flops 20000000000 | tf_op jit(solution)/shard_map/last_image/pallas_call | solution.py:157
Async XLA Ops:
  0.6 26.5 %collective-permute-start.1 = (f32[256,1152]{1,0:T(8,128)}, f32[256,1152]{1,0:T(8,128)S(1)}, u32[]{:S(2)}, u32[]{:S(2)}) collective-permute-start(f32[256,1152]{1,0:T(8,128)} %txt_in.1), channel_id=1, source_target_pairs={{0,510},{1,3},{2,0},{3,5},{4,2},{5,7},{6,4},{7,9},{8,6},{9,11},{10... | collective-permute-start | bytes 3538952 | tf_op jit(solution)/shard_map/ppermute | solution.py:185
  13.6 25.1 %collective-permute-start.3 = (f32[512,1152]{1,0:T(8,128)S(1)}, f32[512,1152]{1,0:T(8,128)S(1)}, u32[]{:S(2)}, u32[]{:S(2)}) collective-permute-start(f32[512,1152]{1,0:T(8,128)S(1)} %get-tuple-element.52), channel_id=1, source_target_pairs={{0,1},{1,0},{2,3},{3,2},{4,5},{5,4},{6,7},{7,6},{8,9},{9,8},{10,11... | collective-permute-start | bytes 7077896 | tf_op jit(solution)/shard_map/ppermute | solution.py:194
  15.6 31.9 %collective-permute-start = (f32[256,1152]{1,0:T(8,128)S(1)}, f32[256,1152]{1,0:T(8,128)S(1)}, u32[]{:S(2)}, u32[]{:S(2)}) collective-permute-start(f32[256,1152]{1,0:T(8,128)S(1)} %get-tuple-element.38.own.refs_2_), channel_id=1, source_target_pairs={{0,510},{1,3},{2,0},{3,5},{4,2},{5,7},{6,4},{7,9},{8,6},{9,11},{10... | collective-permute-start | bytes 3538952 | tf_op jit(solution)/shard_map/ppermute | solution.py:185
  24.0 37.4 %collective-permute-start.5 = (f32[256,1152]{1,0:T(8,128)S(1)}, f32[256,1152]{1,0:T(8,128)S(1)}, u32[]{:S(2)}, u32[]{:S(2)}) collective-permute-start(f32[256,1152]{1,0:T(8,128)S(1)} %get-tuple-element.58.own.refs_3_), channel_id=1, source_target_pairs={{0,2},{1,511},{2,4},{3,1},{4,6},{5,3},{6,8},{7,5},{8,10},{9,7},{10... | collective-permute-start | bytes 3538952 | tf_op jit(solution)/shard_map/ppermute | solution.py:191
  29.5 15.6 %collective-permute-start.2 = (f32[256,1152]{1,0:T(8,128)S(1)}, f32[256,1152]{1,0:T(8,128)S(1)}, u32[]{:S(2)}, u32[]{:S(2)}) collective-permute-start(f32[256,1152]{1,0:T(8,128)S(1)} %get-tuple-element.51), channel_id=1, source_target_pairs={{0,1},{1,0},{2,3},{3,2},{4,5},{5,4},{6,7},{7,6},{8,9},{9,8},{10,11... | collective-permute-start | bytes 3538952 | tf_op jit(solution)/shard_map/ppermute | solution.py:194
  36.8 29.9 %collective-permute-start.8 = (f32[128,1152]{1,0:T(8,128)S(1)}, f32[128,1152]{1,0:T(8,128)S(1)}, u32[]{:S(2)}, u32[]{:S(2)}) collective-permute-start(f32[128,1152]{1,0:T(8,128)S(1)} %get-tuple-element.68), channel_id=1, source_target_pairs={{0,2},{1,511},{2,4},{3,1},{4,6},{5,3},{6,8},{7,5},{8,10},{9,7},{10... | collective-permute-start | bytes 1769480 | tf_op jit(solution)/shard_map/ppermute | solution.py:191
  38.7 29.9 %collective-permute-start.6 = (f32[128,1152]{1,0:T(8,128)S(1)}, f32[128,1152]{1,0:T(8,128)S(1)}, u32[]{:S(2)}, u32[]{:S(2)}) collective-permute-start(f32[128,1152]{1,0:T(8,128)S(1)} %get-tuple-element.66), channel_id=1, source_target_pairs={{0,2},{2,4},{3,1},{4,6},{5,3},{6,8},{7,5},{8,10},{9,7},{10,12},{11... | collective-permute-start | bytes 1769480 | tf_op jit(solution)/shard_map/ppermute | solution.py:191
  47.5 16.9 %collective-permute-start.4 = (f32[256,1152]{1,0:T(8,128)S(1)}, f32[256,1152]{1,0:T(8,128)S(1)}, u32[]{:S(2)}, u32[]{:S(2)}) collective-permute-start(f32[256,1152]{1,0:T(8,128)S(1)} %collective-permute-done.hat), channel_id=1, source_target_pairs={{0,1},{1,0},{2,3},{3,2},{4,5},{5,4},{6,7},{7,6},{8,9},{9,8},{10,11... | collective-permute-start | bytes 3538952 | tf_op jit(solution)/shard_map/ppermute | solution.py:194
  49.9 18.8 %collective-permute-start.7 = (f32[128,1152]{1,0:T(8,128)S(1)}, f32[128,1152]{1,0:T(8,128)S(1)}, u32[]{:S(2)}, u32[]{:S(2)}) collective-permute-start(f32[128,1152]{1,0:T(8,128)S(1)} %get-tuple-element.67), channel_id=1, source_target_pairs={{0,511}} | collective-permute-start | bytes 1769480 | tf_op jit(solution)/shard_map/ppermute | solution.py:250

commit v6 on v5

--- a/solution.py
+++ b/solution.py
@@ -13,7 +13,7 @@
 SMEM = pl.BlockSpec(memory_space=pltpu.SMEM)
 HBM = pl.BlockSpec(memory_space=pltpu.HBM)
 PARTS = 4
-COLUMNS = 256
+COLUMNS = 384
 HINTS = {"last_text": 1, "cross_image": 1, "far_image": 1}
 NT = (((1,), (1,)), ((), ()))
 NN = (((1,), (0,)), ((), ()))

time: 71.1 us -> 71.2 us (level)
  no operation moved by 1% of the time
where the time goes in v6:
time: 71.2 us; the launch traced here: 70.8 us
  starting transfers between devices  41.1 us (58%)
  Pallas kernels  27.4 us (38%)
  between operations  2.26 us (3%)
    pallas_call x10, Pallas kernels, call(): pl.pallas_call(kernel, name=name, out_shape=outs, in_specs=[SMEM] * scala...  27.4 us
    ppermute x2, starting transfers between devices, outward(): lax.ppermute(block, 'dp', [(d, (d + (2 if d % 2 else -2)) % size) for d i...  13.4 us
    ppermute x3, starting transfers between devices, swap(): return lax.ppermute(block, 'dp', [(d, d ^ 1) for d in range(size)])  11.6 us
    ppermute x1, starting transfers between devices, body(): far_img_c = lax.ppermute(passed, 'dp', [(0, size - 1)])  9.2 us
    ppermute x3, starting transfers between devices, inward(): lax.ppermute(block, 'dp', [pair for pair in pairs if pair not in skip])  6.95 us
  transfers between devices with their start and end apart: 9, of which 0 were waited for; matrix products, arithmetic and copies ran while one was open for 0% of the time, Pallas kernels for 36%

profile of v6, /device:TPU:0, one launch (start us, length us, event | category | flops | bytes accessed | tf_op | source)
XLA Modules:
  0.0 70.8 jit_solution(11480439791366267984)
XLA Ops:
  0.6 10.7 %collective-permute-start.1 = (f32[256,1152]{1,0:T(8,128)}, f32[256,1152]{1,0:T(8,128)S(1)}, u32[]{:S(2)}, u32[]{:S(2)}) collective-permute-start(f32[256,1152]{1,0:T(8,128)} %txt_in.1), channel_id=1, source_target_pairs={{0,510},{1,3},{2,0},{3,5},{4,2},{5,7},{6,4},{7,9},{8,6},{9,11},{10... | collective-permute-start | bytes 3538952 | tf_op jit(solution)/shard_map/ppermute | solution.py:185
  11.3 2.3 %unit_rows.1 = (f32[256,1152]{1,0:T(8,128)S(1)}, f32[256,1152]{1,0:T(8,128)S(1)}, f32[512,1152]{1,0:T(8,128)S(1)}, f32[128,1152]{1,0:T(8,128)S(1)}, f32[128,1152...) custom-call(f32[256,1152]{1,0:T(8,128)} %img_in.1, ...), custom_call_target="tpu_custom_call" | custom-call | flops 20000000000 | tf_op jit(solution)/shard_map/unit_rows/pallas_call | solution.py:157
  13.6 1.9 %collective-permute-start.3 = (f32[512,1152]{1,0:T(8,128)S(1)}, f32[512,1152]{1,0:T(8,128)S(1)}, u32[]{:S(2)}, u32[]{:S(2)}) collective-permute-start(f32[512,1152]{1,0:T(8,128)S(1)} %get-tuple-element.52), channel_id=1, source_target_pairs={{0,1},{1,0},{2,3},{3,2},{4,5},{5,4},{6,7},{7,6},{8,9},{9,8},{10,11... | collective-permute-start | bytes 7077896 | tf_op jit(solution)/shard_map/ppermute | solution.py:194
  15.6 2.7 %collective-permute-start = (f32[256,1152]{1,0:T(8,128)S(1)}, f32[256,1152]{1,0:T(8,128)S(1)}, u32[]{:S(2)}, u32[]{:S(2)}) collective-permute-start(f32[256,1152]{1,0:T(8,128)S(1)} %get-tuple-element.38.own.refs_2_), channel_id=1, source_target_pairs={{0,510},{1,3},{2,0},{3,5},{4,2},{5,7},{6,4},{7,9},{8,6},{9,11},{10... | collective-permute-start | bytes 3538952 | tf_op jit(solution)/shard_map/ppermute | solution.py:185
  19.6 4.4 %own_tiles.1 = (f32[256,1152]{1,0:T(8,128)S(1)}, f32[256,1152]{1,0:T(8,128)S(1)}) custom-call(f32[1]{0:T(128)S(6)} %copy.6.scale, f32[1]{0:T(128)S(6)} %copy.7.bias, bf16[256,1152]{1,0:T(8,128)(2,1)S(1)} %get-tuple-element.39.ihi.hi, bf16[256,1152]{1,0:T(8,128)(2,1)S(1)} %get-tuple-element.40.ilo.lo, bf16[256,1152]{1,0:T(8,128)(2,1)S(1)} %get-tuple-element.44.thi.hi, ...), custom_call_target="tpu_custom_call" | custom-call | flops 20000000000 | tf_op jit(solution)/shard_map/own_tiles/pallas_call | solution.py:157
  24.0 3.1 %collective-permute-start.5 = (f32[256,1152]{1,0:T(8,128)S(1)}, f32[256,1152]{1,0:T(8,128)S(1)}, u32[]{:S(2)}, u32[]{:S(2)}) collective-permute-start(f32[256,1152]{1,0:T(8,128)S(1)} %get-tuple-element.58.own.refs_3_), channel_id=1, source_target_pairs={{0,2},{1,511},{2,4},{3,1},{4,6},{5,3},{6,8},{7,5},{8,10},{9,7},{10... | collective-permute-start | bytes 3538952 | tf_op jit(solution)/shard_map/ppermute | solution.py:191
  27.1 0.0 collective-permute-done.1.raw
  27.1 2.4 %near_text.1 = (f32[256,1152]{1,0:T(8,128)S(1)}, f32[256,1152]{1,0:T(8,128)S(1)}) custom-call(f32[1]{0:T(128)S(6)} %copy.6.scale, f32[1]{0:T(128)S(6)} %copy.7.bias, bf16[256,1152]{1,0:T(8,128)(2,1)S(1)} %get-tuple-element.39.ihi.hi, bf16[256,1152]{1,0:T(8,128)(2,1)S(1)} %get-tuple-element.40.ilo.lo, f32[256,1152]{1,0:T(8,128)S(1)} %collective-permute-done.1.raw, ...), custom_call_target="tpu_custom_call" | custom-call | flops 20000000000 | tf_op jit(solution)/shard_map/near_text/pallas_call | solution.py:157
  29.5 7.3 %collective-permute-start.2 = (f32[256,1152]{1,0:T(8,128)S(1)}, f32[256,1152]{1,0:T(8,128)S(1)}, u32[]{:S(2)}, u32[]{:S(2)}) collective-permute-start(f32[256,1152]{1,0:T(8,128)S(1)} %get-tuple-element.51), channel_id=1, source_target_pairs={{0,1},{1,0},{2,3},{3,2},{4,5},{5,4},{6,7},{7,6},{8,9},{9,8},{10,11... | collective-permute-start | bytes 3538952 | tf_op jit(solution)/shard_map/ppermute | solution.py:194
  36.8 1.9 %collective-permute-start.8 = (f32[128,1152]{1,0:T(8,128)S(1)}, f32[128,1152]{1,0:T(8,128)S(1)}, u32[]{:S(2)}, u32[]{:S(2)}) collective-permute-start(f32[128,1152]{1,0:T(8,128)S(1)} %get-tuple-element.68), channel_id=1, source_target_pairs={{0,2},{1,511},{2,4},{3,1},{4,6},{5,3},{6,8},{7,5},{8,10},{9,7},{10... | collective-permute-start | bytes 1769480 | tf_op jit(solution)/shard_map/ppermute | solution.py:191
  38.7 0.0 collective-permute-done.3.both
  38.7 1.9 %collective-permute-start.6 = (f32[128,1152]{1,0:T(8,128)S(1)}, f32[128,1152]{1,0:T(8,128)S(1)}, u32[]{:S(2)}, u32[]{:S(2)}) collective-permute-start(f32[128,1152]{1,0:T(8,128)S(1)} %get-tuple-element.66), channel_id=1, source_target_pairs={{0,2},{2,4},{3,1},{4,6},{5,3},{6,8},{7,5},{8,10},{9,7},{10,12},{11... | collective-permute-start | bytes 1769480 | tf_op jit(solution)/shard_map/ppermute | solution.py:191
  40.7 4.4 %pair_tiles.1 = (f32[256,1152]{1,0:T(8,128)S(1)}, f32[256,1152]{1,0:T(8,128)S(1)}, f32[128,1152]{1,0:T(8,128)S(1)}) custom-call(f32[1]{0:T(128)S(6)} %copy.6.scale, f32[1]{0:T(128)S(6)} %copy.7.bias, bf16[256,1152]{1,0:T(8,128)(2,1)S(1)} %get-tuple-element.39.ihi.hi, bf16[256,1152]{1,0:T(8,128)(2,1)S(1)} %get-tuple-element.40.ilo.lo, ...), custom_call_target="tpu_custom_call" | custom-call | flops 20000000000 | tf_op jit(solution)/shard_map/pair_tiles/pallas_call | solution.py:157
  45.1 0.0 collective-permute-done.2.hat
  45.1 2.4 %cross_text.1 = (f32[256,1152]{1,0:T(8,128)S(1)}, f32[256,1]{1,0:T(8,128)S(1)}) custom-call(f32[1]{0:T(128)S(6)} %copy.6.scale, f32[1]{0:T(128)S(6)} %copy.7.bias, bf16[256,1152]{1,0:T(8,128)(2,1)S(1)} %get-tuple-element.39.ihi.hi, bf16[256,1152]{1,0:T(8,128)(2,1)S(1)} %get-tuple-element.40.ilo.lo, f32[256,1152]{1,0:T(8,128)S(1)} %collective-permute-done.2.hat, ...), custom_call_target="tpu_custom_call" | custom-call | flops 20000000000 | tf_op jit(solution)/shard_map/cross_text/pallas_call | solution.py:157
  47.5 0.0 collective-permute-done.hat
  47.5 2.4 %collective-permute-start.4 = (f32[256,1152]{1,0:T(8,128)S(1)}, f32[256,1152]{1,0:T(8,128)S(1)}, u32[]{:S(2)}, u32[]{:S(2)}) collective-permute-start(f32[256,1152]{1,0:T(8,128)S(1)} %collective-permute-done.hat), channel_id=1, source_target_pairs={{0,1},{1,0},{2,3},{3,2},{4,5},{5,4},{6,7},{7,6},{8,9},{9,8},{10,11... | collective-permute-start | bytes 3538952 | tf_op jit(solution)/shard_map/ppermute | solution.py:194
  49.9 9.2 %collective-permute-start.7 = (f32[128,1152]{1,0:T(8,128)S(1)}, f32[128,1152]{1,0:T(8,128)S(1)}, u32[]{:S(2)}, u32[]{:S(2)}) collective-permute-start(f32[128,1152]{1,0:T(8,128)S(1)} %get-tuple-element.67), channel_id=1, source_target_pairs={{0,511}} | collective-permute-start | bytes 1769480 | tf_op jit(solution)/shard_map/ppermute | solution.py:250
  59.1 2.3 %near_image.1.grad = f32[256,1152]{1,0:T(8,128)S(1)} custom-call(f32[1]{0:T(128)S(6)} %copy.6.scale, f32[1]{0:T(128)S(6)} %copy.7.bias, bf16[256,1152]{1,0:T(8,128)(2,1)S(1)} %get-tuple-element.44.thi.hi, bf16[256,1152]{1,0:T(8,128)(2,1)S(1)} %get-tuple-element.45.tlo.lo, f32[256,1152]{1,0:T(8,128)S(1)} %collective-permute-done.hat, ...), custom_call_target="tpu_custom_call" | custom-call | flops 20000000000 | tf_op jit(solution)/shard_map/near_image/pallas_call | solution.py:157
  61.4 0.0 collective-permute-done.5.refs_0_
  61.4 3.2 %last_text.1 = f32[256,1152]{1,0:T(8,128)} custom-call(f32[1]{0:T(128)S(6)} %copy.6.scale, f32[1]{0:T(128)S(6)} %copy.7.bias, bf16[256,1152]{1,0:T(8,128)(2,1)S(1)} %get-tuple-element.39.ihi.hi, bf16[256,1152]{1,0:T(8,128)(2,1)S(1)} %get-tuple-element.40.ilo.lo, f32[256,1152]{1,0:T(8,128)S(1)} %collective-permute-done.5.refs_0_, ...), custom_call_target="tpu_custom_call" | custom-call | flops 1 | tf_op jit(solution)/shard_map/last_text/pallas_call | solution.py:157
  64.6 0.0 collective-permute-done.4.hat
  64.6 2.3 %cross_image.1.grad = f32[256,1152]{1,0:T(8,128)S(1)} custom-call(f32[1]{0:T(128)S(6)} %copy.6.scale, f32[1]{0:T(128)S(6)} %copy.7.bias, bf16[256,1152]{1,0:T(8,128)(2,1)S(1)} %get-tuple-element.44.thi.hi, bf16[256,1152]{1,0:T(8,128)(2,1)S(1)} %get-tuple-element.45.tlo.lo, f32[256,1152]{1,0:T(8,128)S(1)} %collective-permute-done.4.hat, ...), custom_call_target="tpu_custom_call" | custom-call | flops 1 | tf_op jit(solution)/shard_map/cross_image/pallas_call | solution.py:157
  66.9 0.0 collective-permute-done.8.hat
  66.9 1.9 %far_image.1 = (f32[256,1152]{1,0:T(8,128)S(1)}, f32[256,1]{1,0:T(8,128)S(1)}) custom-call(f32[1]{0:T(128)S(6)} %copy.6.scale, f32[1]{0:T(128)S(6)} %copy.7.bias, bf16[256,1152]{1,0:T(8,128)(2,1)S(1)} %get-tuple-element.44.thi.hi, bf16[256,1152]{1,0:T(8,128)(2,1)S(1)} %get-tuple-element.45.tlo.lo, f32[128,1152]{1,0:T(8,128)S(1)} %collective-permute-done.8.hat, ...), custom_call_target="tpu_custom_call" | custom-call | flops 1 | tf_op jit(solution)/shard_map/far_image/pallas_call | solution.py:157
  68.8 0.0 collective-permute-done.6.refs_0_
  68.8 0.0 collective-permute-done.7.refs_1_
  68.8 1.8 %last_image.1 = f32[256,1152]{1,0:T(8,128)} custom-call(f32[1]{0:T(128)S(6)} %copy.6.scale, f32[1]{0:T(128)S(6)} %copy.7.bias, bf16[256,1152]{1,0:T(8,128)(2,1)S(1)} %get-tuple-element.44.thi.hi, bf16[256,1152]{1,0:T(8,128)(2,1)S(1)} %get-tuple-element.45.tlo.lo, f32[128,1152]{1,0:T(8,128)S(1)} %collective-permute-done.6.refs_0_, ...), custom_call_target="tpu_custom_call" | custom-call | flops 20000000000 | tf_op jit(solution)/shard_map/last_image/pallas_call | solution.py:157
Async XLA Ops:
  0.6 26.5 %collective-permute-start.1 = (f32[256,1152]{1,0:T(8,128)}, f32[256,1152]{1,0:T(8,128)S(1)}, u32[]{:S(2)}, u32[]{:S(2)}) collective-permute-start(f32[256,1152]{1,0:T(8,128)} %txt_in.1), channel_id=1, source_target_pairs={{0,510},{1,3},{2,0},{3,5},{4,2},{5,7},{6,4},{7,9},{8,6},{9,11},{10... | collective-permute-start | bytes 3538952 | tf_op jit(solution)/shard_map/ppermute | solution.py:185
  13.6 25.1 %collective-permute-start.3 = (f32[512,1152]{1,0:T(8,128)S(1)}, f32[512,1152]{1,0:T(8,128)S(1)}, u32[]{:S(2)}, u32[]{:S(2)}) collective-permute-start(f32[512,1152]{1,0:T(8,128)S(1)} %get-tuple-element.52), channel_id=1, source_target_pairs={{0,1},{1,0},{2,3},{3,2},{4,5},{5,4},{6,7},{7,6},{8,9},{9,8},{10,11... | collective-permute-start | bytes 7077896 | tf_op jit(solution)/shard_map/ppermute | solution.py:194
  15.6 31.9 %collective-permute-start = (f32[256,1152]{1,0:T(8,128)S(1)}, f32[256,1152]{1,0:T(8,128)S(1)}, u32[]{:S(2)}, u32[]{:S(2)}) collective-permute-start(f32[256,1152]{1,0:T(8,128)S(1)} %get-tuple-element.38.own.refs_2_), channel_id=1, source_target_pairs={{0,510},{1,3},{2,0},{3,5},{4,2},{5,7},{6,4},{7,9},{8,6},{9,11},{10... | collective-permute-start | bytes 3538952 | tf_op jit(solution)/shard_map/ppermute | solution.py:185
  24.0 37.4 %collective-permute-start.5 = (f32[256,1152]{1,0:T(8,128)S(1)}, f32[256,1152]{1,0:T(8,128)S(1)}, u32[]{:S(2)}, u32[]{:S(2)}) collective-permute-start(f32[256,1152]{1,0:T(8,128)S(1)} %get-tuple-element.58.own.refs_3_), channel_id=1, source_target_pairs={{0,2},{1,511},{2,4},{3,1},{4,6},{5,3},{6,8},{7,5},{8,10},{9,7},{10... | collective-permute-start | bytes 3538952 | tf_op jit(solution)/shard_map/ppermute | solution.py:191
  29.5 15.6 %collective-permute-start.2 = (f32[256,1152]{1,0:T(8,128)S(1)}, f32[256,1152]{1,0:T(8,128)S(1)}, u32[]{:S(2)}, u32[]{:S(2)}) collective-permute-start(f32[256,1152]{1,0:T(8,128)S(1)} %get-tuple-element.51), channel_id=1, source_target_pairs={{0,1},{1,0},{2,3},{3,2},{4,5},{5,4},{6,7},{7,6},{8,9},{9,8},{10,11... | collective-permute-start | bytes 3538952 | tf_op jit(solution)/shard_map/ppermute | solution.py:194
  36.8 30.1 %collective-permute-start.8 = (f32[128,1152]{1,0:T(8,128)S(1)}, f32[128,1152]{1,0:T(8,128)S(1)}, u32[]{:S(2)}, u32[]{:S(2)}) collective-permute-start(f32[128,1152]{1,0:T(8,128)S(1)} %get-tuple-element.68), channel_id=1, source_target_pairs={{0,2},{1,511},{2,4},{3,1},{4,6},{5,3},{6,8},{7,5},{8,10},{9,7},{10... | collective-permute-start | bytes 1769480 | tf_op jit(solution)/shard_map/ppermute | solution.py:191
  38.7 30.1 %collective-permute-start.6 = (f32[128,1152]{1,0:T(8,128)S(1)}, f32[128,1152]{1,0:T(8,128)S(1)}, u32[]{:S(2)}, u32[]{:S(2)}) collective-permute-start(f32[128,1152]{1,0:T(8,128)S(1)} %get-tuple-element.66), channel_id=1, source_target_pairs={{0,2},{2,4},{3,1},{4,6},{5,3},{6,8},{7,5},{8,10},{9,7},{10,12},{11... | collective-permute-start | bytes 1769480 | tf_op jit(solution)/shard_map/ppermute | solution.py:191
  47.5 17.1 %collective-permute-start.4 = (f32[256,1152]{1,0:T(8,128)S(1)}, f32[256,1152]{1,0:T(8,128)S(1)}, u32[]{:S(2)}, u32[]{:S(2)}) collective-permute-start(f32[256,1152]{1,0:T(8,128)S(1)} %collective-permute-done.hat), channel_id=1, source_target_pairs={{0,1},{1,0},{2,3},{3,2},{4,5},{5,4},{6,7},{7,6},{8,9},{9,8},{10,11... | collective-permute-start | bytes 3538952 | tf_op jit(solution)/shard_map/ppermute | solution.py:194
  49.9 19.0 %collective-permute-start.7 = (f32[128,1152]{1,0:T(8,128)S(1)}, f32[128,1152]{1,0:T(8,128)S(1)}, u32[]{:S(2)}, u32[]{:S(2)}) collective-permute-start(f32[128,1152]{1,0:T(8,128)S(1)} %get-tuple-element.67), channel_id=1, source_target_pairs={{0,511}} | collective-permute-start | bytes 1769480 | tf_op jit(solution)/shard_map/ppermute | solution.py:250
